TPU v7x, 768 devices: a whole 4x8x12 slice. The times are simulated.
768 devices in a mesh: wide: 12 (over z_lo, core), narrow: 64 (over x, z_hi, y).
Axes of the slice: x: 4, y: 8, z: 12 (z_hi: 2, z_lo: 6; z = z_hi * 6 + z_lo), core: 2. Of those that a mesh axis runs over, the one named last changes fastest.
Arguments:
- grad_parts: bfloat16 [12, 3584, 8192], P('wide', 'narrow'), may hold values from -6 to 6
- master: bfloat16 [3584, 8192], P('narrow'), may hold values from -0.1875 to 0.1875
- moment_one: float32 [3584, 8192], P('narrow'), may hold values from -4 to 4
- moment_two: float32 [3584, 8192], P('narrow'), may hold values from 0.01 to 1
- gate_up: bfloat16 [3584, 2, 8192], P(None, None, 'narrow'), may hold values from -0.09375 to 0.09375
- tokens: bfloat16 [1536, 3584], P(('wide', 'narrow')), may hold values from -6 to 6
- expert_ids: int32 [1536, 4], P(('wide', 'narrow')), may hold values from 0 to 7, all different within a row; in each aligned block of 2 rows (0 to 1, 2 to 3, ...) at most 2 rows name the same one
- gate_vals: bfloat16 [1536, 4], P(('wide', 'narrow')), may hold values from 0.049804688 to 1
Outputs:
- new_master: bfloat16 [3584, 8192], P('narrow')
- new_one: float32 [3584, 8192], P('narrow')
- new_two: float32 [3584, 8192], P('narrow')
- combined: bfloat16 [1536, 3584], P(('wide', 'narrow'))
Inputs may be any that keep to these rules, and one draw needn't show every extreme that they name: `expert_ids`: each token names 4 distinct experts; each device's 2 tokens name every expert at most 2 times (which follows from the distinct ids), and some device names one expert twice.
All inputs are finite; a program needn't handle non-finite values.
Results may differ from a plain program's by a relative error of at most 0.022.
Values may be sent and summed in bfloat16 or wider, within the bound.
A program may use at most 64 MiB of HBM per device.

v0:
```python
import jax
import jax.numpy as jnp
from jax import lax
from jax.sharding import PartitionSpec as P

EXPERTS = 8
QBLOCK = 128


beta_first = 0.9
beta_second = 0.95
learn_rate = 0.003
adam_eps = 1e-08
quant_limit = 448.0
amax_eps = 1e-06
bias_first = 1.0 - 0.9**10
bias_second = 1.0 - 0.95**10


def adam_quant(grad_sum, master, moment_one, moment_two):
    new_one = beta_first * moment_one + (1.0 - beta_first) * grad_sum
    new_two = beta_second * moment_two + (1.0 - beta_second) * grad_sum * grad_sum
    step_dir = new_one / bias_first / (jnp.sqrt(new_two / bias_second) + adam_eps)
    updated = master.astype(jnp.float32) - learn_rate * step_dir
    row_count, col_count = updated.shape
    blocks = updated.reshape(row_count, col_count // QBLOCK, QBLOCK)
    scales = ((jnp.max(jnp.abs(blocks), axis=2) + amax_eps) / quant_limit).astype(jnp.bfloat16)
    quanta = (
        (blocks / scales.astype(jnp.float32)[:, :, None])
        .astype(jnp.bfloat16)
        .reshape(row_count, col_count)
    )
    return (updated.astype(jnp.bfloat16), new_one, new_two, quanta, scales)


def expert_rows(rows_in, gate_piece, quanta, scales):
    unit_count = gate_piece.shape[2]
    proj_both = jnp.dot(
        rows_in,
        gate_piece.reshape(gate_piece.shape[0], 2 * unit_count),
        preferred_element_type=jnp.float32,
    )
    hidden = (jax.nn.silu(proj_both[:, :unit_count]) * proj_both[:, unit_count:]).astype(
        jnp.bfloat16
    )
    block_count = unit_count // QBLOCK
    per_block = jnp.einsum(
        "rbf,dbf->rbd",
        hidden.reshape(-1, block_count, QBLOCK),
        quanta.reshape(quanta.shape[0], block_count, QBLOCK),
        preferred_element_type=jnp.float32,
    )
    return jnp.einsum("rbd,db->rd", per_block, scales.astype(jnp.float32))


def body(grad_parts, master, moment_one, moment_two, gate_up, tokens, expert_ids, gate_vals):
    grad_sum = lax.psum(grad_parts[0], "wide").astype(jnp.float32)
    new_master, new_one, new_two, quanta, scales = adam_quant(
        grad_sum, master, moment_one, moment_two
    )
    owned_q, owned_s = (
        lax.all_to_all(quanta, "narrow", split_axis=1, concat_axis=0, tiled=True),
        lax.all_to_all(scales, "narrow", split_axis=1, concat_axis=0, tiled=True),
    )
    onehot = (expert_ids[:, :, None] == jnp.arange(EXPERTS, dtype=jnp.int32)[None, None, :]).astype(
        jnp.float32
    )
    gate_float = gate_vals.astype(jnp.float32)
    group_size = lax.axis_size("narrow") // EXPERTS
    weights_tok = jnp.sum(onehot * gate_float[:, :, None], axis=1).astype(jnp.bfloat16)
    all_tokens, all_weights = (
        lax.all_gather(tokens, "narrow", axis=0, tiled=True),
        lax.all_gather(weights_tok, "narrow", axis=0, tiled=True),
    )
    own_expert = lax.axis_index("narrow") // group_size
    chosen = (jnp.arange(EXPERTS, dtype=jnp.int32) == own_expert).astype(jnp.float32)
    own_weight = jnp.sum(all_weights.astype(jnp.float32) * chosen[None, :], axis=1)
    partial_value = (
        expert_rows(all_tokens, gate_up, owned_q, owned_s).astype(jnp.bfloat16).astype(jnp.float32)
    )
    combined = lax.psum_scatter(
        own_weight[:, None] * partial_value, "narrow", scatter_dimension=0, tiled=True
    )
    return (new_master, new_one, new_two, combined.astype(jnp.bfloat16))


def solution(mesh):
    in_specs = (
        P("wide", "narrow", None),
        P("narrow", None),
        P("narrow", None),
        P("narrow", None),
        P(None, None, "narrow"),
        P(("wide", "narrow"), None),
        P(("wide", "narrow"), None),
        P(("wide", "narrow"), None),
    )
    out_specs = (
        P("narrow", None),
        P("narrow", None),
        P("narrow", None),
        P(("wide", "narrow"), None),
    )
    return jax.shard_map(body, mesh=mesh, in_specs=in_specs, out_specs=out_specs, check_vma=False)
```

profile of v0, /device:TPU:64, one launch (start us, length us, event | category | flops | bytes accessed | tf_op | source)
XLA Modules:
  0.0 1267.8 jit_solution(12440429605677853665)
XLA Ops:
  7.2 0.0 all-reduce.4.cloned.1.call-start
  7.2 0.7 all-reduce.4.cloned.1.call-update
  7.9 143.8 %all-reduce.4.cloned.1.call-done = bf16[56,8192]{1,0:T(8,128)(2,1)} async-done(((bf16[56,8192]{1,0:T(8,128)(2,1)}), bf16[56,8192]{1,0:T(8,128)(2,1)}) %all-reduce.4.cloned.1.call-update) | async-done | bytes 917520 | tf_op jit(solution)/shard_map/psum | solution.py:57
  151.7 6.0 abs_bitcast_fusion
  157.7 0.3 copy.27
  158.0 0.5 reduce_max.9
  158.6 0.0 copy-start
  158.6 0.7 copy.21
  159.3 15.9 %all-to-all-start = ((bf16[56,64,1]{0,2,1:T(2,128)(2,1)}), bf16[56,64,1]{0,2,1:T(2,128)(2,1)S(1)}, u32[]{:S(2)}, u32[]{:S(2)}) async-start(bf16[56,64,1]{0,2,1:T(2,128)(2,1)} %copy.21), calls=%async_computation | async-start | bytes 65536 | tf_op jit(solution)/shard_map/all_to_all | solution.py:63
  175.3 0.5 div.54
  175.8 0.0 copy-done
  175.8 2.2 fusion.10
  178.0 0.0 copy-start.3
  178.0 0.0 copy-start.1
  178.0 1.1 copy.38
  179.1 12.8 %all-to-all-done = bf16[56,64,1]{0,2,1:T(2,128)(2,1)S(1)} async-done(((bf16[56,64,1]{0,2,1:T(2,128)(2,1)}), bf16[56,64,1]{0,2,1:T(2,128)(2,1)S(1)}, u32[]{:S(2)}, u32[]{:S(2)}) %all-to-all-start) | async-done | bytes 7200 | tf_op jit(solution)/shard_map/all_to_all | solution.py:63
  192.0 4.7 all-to-all-start.1
  196.7 0.0 copy-start.2
  196.7 0.0 copy-done.3
  196.8 0.0 copy-done.1
  196.8 278.3 %all-gather.1 = bf16[64,2,3584]{2,1,0:T(2,128)(2,1)S(1)} all-gather(bf16[1,2,3584]{2,1,0:T(2,128)(2,1)S(1)} %bitcast.45), channel_id=1, replica_groups=mesh['wide'=12,'narrow'=64] {'narrow'}, dimensions={0}, use_global_device_ids=true | all-gather | bytes 931840 | tf_op jit(solution)/shard_map/all_gather | solution.py:72
  475.0 0.3 reshape.74
  475.4 1.3 dynamic-slice
  477.3 0.0 copy-done.2
  477.3 0.1 select_reduce_fusion
  477.4 250.0 %all-gather = bf16[64,2,8]{2,1,0:T(2,128)(2,1)S(1)} all-gather(bf16[1,2,8]{2,1,0:T(2,128)(2,1)S(1)} %bitcast.46), channel_id=1, replica_groups=mesh['wide'=12,'narrow'=64] {'narrow'}, dimensions={0}, use_global_device_ids=true | all-gather | bytes 2080 | tf_op jit(solution)/shard_map/all_gather | solution.py:73
  727.4 0.1 fusion.12
  727.6 1.9 fusion.6
  729.5 0.1 bitcast_reduce_fusion
  729.6 0.1 reshape.70
  729.7 0.0 all-to-all-done.1
  729.7 0.5 fusion.3
  730.2 529.5 %all-reduce.5 = bf16[128,3584]{0,1:T(8,128)(2,1)S(1)} all-reduce(f32[128,3584]{0,1:T(8,128)S(1)} %fusion.3), channel_id=2, replica_groups=mesh['wide'=12,'narrow'=64] {'narrow'}, use_global_device_ids=true, to_apply=%region_4.5.clone | all-reduce | flops 458752 | bytes 2752512
  1259.7 0.3 dynamic-slice_convert_fusion
  1260.0 0.9 copy.23
  (3 shorter events, 0.0 us)
Async XLA Ops:
  7.2 144.6 %all-reduce.4.cloned.1.call-start = ((), (), s32[]{:S(2)}) async-start(), calls=%async_computation.2 | async-start | bytes 1835008 | tf_op jit(solution)/shard_map/psum | solution.py:57
  158.6 17.2 %copy-start = (f32[56,8192]{1,0:T(8,128)S(1)}, f32[56,8192]{1,0:T(8,128)}, u32[]{:S(2)}) copy-start(f32[56,8192]{1,0:T(8,128)} %get-tuple-element.25) | copy-start | bytes 5505028
  159.3 32.6 %all-to-all-start = ((bf16[56,64,1]{0,2,1:T(2,128)(2,1)}), bf16[56,64,1]{0,2,1:T(2,128)(2,1)S(1)}, u32[]{:S(2)}, u32[]{:S(2)}) async-start(bf16[56,64,1]{0,2,1:T(2,128)(2,1)} %copy.21), calls=%async_computation | async-start | bytes 65536 | tf_op jit(solution)/shard_map/all_to_all | solution.py:63
  178.0 18.7 %copy-start.3 = (bf16[2,4]{1,0:T(2,128)(2,1)S(1)}, bf16[2,4]{1,0:T(2,128)(2,1)}, u32[]{:S(2)}) copy-start(bf16[2,4]{1,0:T(2,128)(2,1)} %param.15) | copy-start | bytes 52
  178.0 18.7 %copy-start.1 = (bf16[2,3584]{1,0:T(2,128)(2,1)S(1)}, bf16[2,3584]{1,0:T(2,128)(2,1)}, u32[]{:S(2)}) copy-start(bf16[2,3584]{1,0:T(2,128)(2,1)} %param.13) | copy-start | bytes 43012
  192.0 537.7 %all-to-all-start.1 = ((bf16[56,64,128]{2,0,1:T(8,128)(2,1)}), bf16[56,64,128]{2,0,1:T(8,128)(2,1)S(1)}, u32[]{:S(2)}, u32[]{:S(2)}) async-start(bf16[56,64,128]{2,0,1:T(8,128)(2,1)} %bitcast.39), calls=%async_computation.1 | async-start | bytes 1835008 | tf_op jit(solution)/shard_map/all_to_all | solution.py:62
  196.7 280.6 %copy-start.2 = (s32[2,4]{1,0:T(2,128)S(1)}, s32[2,4]{1,0:T(2,128)}, u32[]{:S(2)}) copy-start(s32[2,4]{1,0:T(2,128)} %param.14) | copy-start | bytes 100
Sparse Core Ops, SparseCore 0:
  11.2 140.4 all-reduce.3
where the time goes:
time: 1270 us
  blocking collectives  1060 us (83%)
  waiting for transfers between devices  157 us (12%)
  starting transfers between devices  20.7 us (2%)
  between operations  14.9 us (1%)
    unnamed x1, blocking collectives  529 us
    all_gather x1, blocking collectives, body(): lax.all_gather(tokens, 'narrow', axis=0, tiled=True)  278 us
    all_gather x1, blocking collectives, body(): lax.all_gather(weights_tok, 'narrow', axis=0, tiled=True)  250 us
    psum x1, waiting for transfers between devices, body(): grad_sum = lax.psum(grad_parts[0], 'wide').astype(jnp.float32)  144 us
  transfers between devices with their start and end apart: 3, of which 2 were waited for; matrix products, arithmetic and copies ran while one was open for 1% of the time, Pallas kernels for 0%

commit v1 on v0

v1 whole, which is shorter than its diff:
```python
import jax
import jax.numpy as jnp
from jax import lax
from jax.experimental import pallas as pl
from jax.experimental.pallas import tpu as pltpu
from jax.sharding import PartitionSpec as P

EXPERTS = 8
QBLOCK = 128
X, ZH, Y = 4, 2, 8
XZ = X * ZH
ZL = 6
CHUNKS = 8

beta_first = 0.9
beta_second = 0.95
learn_rate = 0.003
adam_eps = 1e-08
quant_limit = 448.0
amax_eps = 1e-06
bias_first = 1.0 - 0.9**10
bias_second = 1.0 - 0.95**10

VMEM = pl.BlockSpec(memory_space=pltpu.VMEM)
DMA = pltpu.SemaphoreType.DMA
f32 = jnp.float32
bf16 = jnp.bfloat16


def at_narrow(index):
    return {"narrow": index}


def at_wide(index):
    return {"wide": index}


def greet(partners):
    barrier = pltpu.get_barrier_semaphore()
    for where in partners:
        pl.semaphore_signal(barrier, inc=1, device_id=where, device_id_type=pl.DeviceIdType.MESH)
    pl.semaphore_wait(barrier, len(partners))


def remote(src, dst, send, recv, where):
    return pltpu.make_async_remote_copy(
        src_ref=src,
        dst_ref=dst,
        send_sem=send,
        recv_sem=recv,
        device_id=where,
        device_id_type=pl.DeviceIdType.MESH,
    )


def place():
    n = lax.axis_index("narrow")
    return n // (ZH * Y), (n // Y) % ZH, n % Y


def narrow_of(x, zh, y):
    return at_narrow((x * ZH + zh) * Y + y)


def gather_xz(own, landing, sems, x, zh, y):
    me = x * ZH + zh
    local = pltpu.make_async_copy(own, landing.at[me], sems.at[8])
    local.start()
    copy = remote(own, landing.at[me], sems.at[0], sems.at[1], narrow_of(x, 1 - zh, y))
    copy.start()
    local.wait()
    copy.wait()
    pair = landing.at[pl.ds(x * ZH, ZH)]
    copies = []
    for k in range(1, X):
        copies.append(
            remote(pair, pair, sems.at[1 + k], sems.at[4 + k], narrow_of((x + k) % X, zh, y))
        )
        copies[-1].start()
    for copy in copies:
        copy.wait()


def ring_y(blocks, right_send, right_recv, left_send, left_recv, x, zh, y):
    right = narrow_of(x, zh, (y + 1) % Y)
    left = narrow_of(x, zh, (y + Y - 1) % Y)
    for s in range(Y // 2):
        there = blocks.at[(y + Y - s) % Y]
        going = [remote(there, there, right_send.at[s], right_recv.at[s], right)]
        if s < Y // 2 - 1:
            there = blocks.at[(y + s) % Y]
            going.append(remote(there, there, left_send.at[s], left_recv.at[s], left))
        for copy in going:
            copy.start()
        for copy in going:
            copy.wait()


GATHER_SEMS = [DMA((9,)), DMA((4,)), DMA((4,)), DMA((3,)), DMA((3,))]


def partners_of(x, zh, y):
    found = [narrow_of(x, 1 - zh, y)]
    found += [narrow_of((x + k) % X, zh, y) for k in range(1, X)]
    return found + [narrow_of(x, zh, (y + k) % Y) for k in (1, Y - 1)]


def tokens_kernel(own_ref, out_ref, landing, wide_rows, sems, rs, rr, ls, lr):
    x, zh, y = place()
    greet(partners_of(x, zh, y))
    gather_xz(own_ref, landing, sems, x, zh, y)
    for j in range(XZ):
        for i in range(2):
            wide_rows[i * XZ + j : i * XZ + j + 1, :] = landing[j, i : i + 1, :].astype(f32)
    out_ref[pl.ds(y, 1)] = wide_rows[...].astype(bf16)[None]
    ring_y(out_ref, rs, rr, ls, lr, x, zh, y)


def hidden_kernel(own_ref, out_ref, sems, rs, rr, ls, lr):
    x, zh, y = place()
    greet(partners_of(x, zh, y))
    gather_xz(own_ref, out_ref.at[y], sems, x, zh, y)
    ring_y(out_ref, rs, rr, ls, lr, x, zh, y)


def grads_kernel(g_ref, out_ref, pre, land, part, ps, pr, is_, ir, os_, or_, cs, cr):
    w = lax.axis_index("wide")
    zl, core = w // 2, w % 2
    rows, columns = g_ref.shape
    half = columns // 2
    size = half // CHUNKS
    low = zl < ZL // 2
    edge = (zl == 0) | (zl == ZL - 1)
    mid = (zl == ZL // 2 - 1) | (zl == ZL // 2)
    inner = jnp.logical_not(edge | mid)
    inward = at_wide(jnp.where(low, w + 2, w - 2))
    outward = at_wide(jnp.where(edge, w, jnp.where(low, w - 2, w + 2)))
    other = at_wide(w + 1 - 2 * core)

    barrier = pltpu.get_barrier_semaphore()

    def signal(where):
        pl.semaphore_signal(barrier, inc=1, device_id=where, device_id_type=pl.DeviceIdType.MESH)

    signal(inward)
    signal(other)

    @pl.when(jnp.logical_not(edge))
    def _():
        signal(outward)

    pl.semaphore_wait(barrier, jnp.where(edge, 2, 3))

    def span(core_of, k):
        return pl.ds(pl.multiple_of(core_of * half + k * size, size), size)

    def here(k):
        return pl.ds(k * size, size)

    def pre_copy(k):
        return remote(g_ref.at[:, span(1 - core, k)], pre.at[:, here(k)], ps.at[k], pr.at[k], other)

    to_slot = jnp.where(mid, 1, 0)

    def in_copy(k, slot):
        return remote(part.at[:, here(k)], land.at[slot, :, here(k)], is_.at[k], ir.at[slot, k], inward)

    def out_copy(k):
        cut = out_ref.at[:, span(core, k)]
        return remote(cut, cut, os_.at[k], or_.at[k], outward)

    def core_copy(k, which):
        cut = out_ref.at[:, span(which, k)]
        return remote(cut, cut, cs.at[k], cr.at[k], other)

    for k in range(CHUNKS):
        pre_copy(k).start()

    def inbound(k):
        pre_copy(k).wait_recv()
        total = g_ref[:, span(core, k)].astype(f32) + pre[:, here(k)].astype(f32)

        @pl.when(edge)
        def _():
            part[:, here(k)] = total.astype(bf16)

        @pl.when(jnp.logical_not(edge))
        def _():
            in_copy(k, 0).wait_recv()
            part[:, here(k)] = (total + land[0, :, here(k)].astype(f32)).astype(bf16)

        in_copy(k, to_slot).start()

    def outbound_mid(k):
        in_copy(k, 1).wait_recv()
        total = part[:, here(k)].astype(f32) + land[1, :, here(k)].astype(f32)
        out_ref[:, span(core, k)] = total.astype(bf16)
        out_copy(k).start()
        core_copy(k, core).start()

    def outbound_inner(k):
        out_copy(k).wait_recv()
        out_copy(k).start()
        core_copy(k, core).start()

    def outbound_edge(k):
        out_copy(k).wait_recv()
        core_copy(k, core).start()

    for s in range(CHUNKS + 5):
        if s < CHUNKS:
            inbound(s)
        for role, lag, step in ((mid, 1, outbound_mid), (inner, 3, outbound_inner), (edge, 5, outbound_edge)):
            if 0 <= s - lag < CHUNKS:
                pl.when(role)(lambda step=step, k=s - lag: step(k))

    for k in range(CHUNKS):
        core_copy(k, 1 - core).wait_recv()
        pre_copy(k).wait_send()
        in_copy(k, to_slot).wait_send()
        core_copy(k, core).wait_send()

    @pl.when(jnp.logical_not(edge))
    def _():
        for k in range(CHUNKS):
            out_copy(k).wait_send()


def adam_kernel(g_ref, p_ref, one_ref, two_ref, hid_ref, newp_ref, newone_ref, newtwo_ref, comb_ref, acc):
    step = pl.program_id(0)
    rows = g_ref.shape[0]

    @pl.when(step == 0)
    def _():
        acc[...] = jnp.zeros_like(acc)

    total = acc[:rows, :]
    for b in range(Y):
        cut = slice(b * QBLOCK, (b + 1) * QBLOCK)
        grad = g_ref[:, cut].astype(f32)
        one = beta_first * one_ref[:, cut] + (1.0 - beta_first) * grad
        two = beta_second * two_ref[:, cut] + (1.0 - beta_second) * grad * grad
        newone_ref[:, cut] = one
        newtwo_ref[:, cut] = two
        step_dir = one * (1.0 / bias_first) / (jnp.sqrt(two * (1.0 / bias_second)) + adam_eps)
        updated = p_ref[:, cut].astype(f32) - learn_rate * step_dir
        newp_ref[:, cut] = updated.astype(bf16)
        amax = jnp.max(jnp.abs(updated), axis=1, keepdims=True)
        scale = ((amax + amax_eps) / quant_limit).astype(bf16).astype(f32)
        quanta = (updated * (1.0 / scale)).astype(bf16)
        total += scale * jnp.dot(quanta, hid_ref[b, 0], preferred_element_type=f32)
    acc[:rows, :] = total

    @pl.when(step == pl.num_programs(0) - 1)
    def _():
        turned = jnp.transpose(acc[...])
        for j in range(Y):
            first = turned[j * 16 : j * 16 + 8]
            second = turned[j * 16 + 8 : j * 16 + 16]
            comb_ref[j] = jnp.concatenate([first, second], axis=1)


def deliver_kernel(comb_ref, out_ref, first, turned, s1, r1, s2, r2):
    x, zh, y = place()
    me = x * ZH + zh
    partners = [narrow_of(x, zh, (y + k) % Y) for k in range(1, Y)]
    others = [(me + k) % XZ for k in range(1, XZ)]
    partners += [at_narrow(j * Y + y) for j in others]
    greet(partners)
    copies = []
    for k in range(1, Y):
        to = (y + k) % Y
        copies.append(remote(comb_ref.at[to], first.at[y], s1.at[k], r1.at[k], narrow_of(x, zh, to)))
        copies[-1].start()
    first[pl.ds(y, 1)] = comb_ref[pl.ds(y, 1)]
    for copy in copies:
        copy.wait()
    for j in range(Y):
        turned[:, j, :] = first[j]
    copies = []
    for k, to in enumerate(others):
        copies.append(remote(turned.at[to], out_ref.at[me], s2.at[k], r2.at[k], at_narrow(to * Y + y)))
        copies[-1].start()
    out_ref[pl.ds(me, 1)] = turned[pl.ds(me, 1)]
    for copy in copies:
        copy.wait()


def comm(kernel, out_shape, scratch, number):
    return pl.pallas_call(
        kernel,
        out_shape=out_shape,
        in_specs=[VMEM],
        out_specs=VMEM,
        scratch_shapes=scratch,
        compiler_params=pltpu.CompilerParams(
            collective_id=number, has_side_effects=True, vmem_limit_bytes=40 * 2**20
        ),
    )


def body(grad_parts, master, moment_one, moment_two, gate_up, tokens, expert_ids, gate_vals):
    shape = jax.ShapeDtypeStruct
    rows, columns = master.shape
    width = tokens.shape[1]
    onehot = expert_ids[:, :, None] == jnp.arange(EXPERTS, dtype=jnp.int32)[None, None, :]
    weights = jnp.sum(jnp.where(onehot, gate_vals.astype(f32)[:, :, None], 0.0), axis=1).astype(bf16)
    packed = jnp.concatenate([tokens, jnp.pad(weights, ((0, 0), (0, QBLOCK - EXPERTS)))], axis=1)
    full = width + QBLOCK
    gathered = comm(
        tokens_kernel,
        shape((Y, 16, full), bf16),
        [pltpu.VMEM((XZ, 2, full), bf16), pltpu.VMEM((16, full), f32)] + GATHER_SEMS,
        0,
    )(packed).reshape(Y * 16, full)

    proj = jnp.dot(gathered[:, :width], gate_up.reshape(width, 2 * QBLOCK), preferred_element_type=f32)
    expert = lax.axis_index("narrow") // Y
    chosen = jnp.arange(EXPERTS, dtype=jnp.int32) == expert
    weight = jnp.sum(jnp.where(chosen[None, :], gathered[:, width : width + EXPERTS].astype(f32), 0.0), axis=1)
    hidden = weight[:, None] * jax.nn.silu(proj[:, :QBLOCK]) * proj[:, QBLOCK:]
    hidden = hidden.astype(bf16).T
    tok = hidden.shape[1]
    hid_all = comm(hidden_kernel, shape((Y, XZ, QBLOCK, tok), bf16), GATHER_SEMS, 1)(hidden)

    half = columns // 2
    sem = DMA((CHUNKS,))
    grad = comm(
        grads_kernel,
        shape((rows, columns), bf16),
        [
            pltpu.VMEM((rows, half), bf16),
            pltpu.VMEM((2, rows, half), bf16),
            pltpu.VMEM((rows, half), bf16),
            sem, sem, sem, DMA((2, CHUNKS)), sem, sem, sem, sem,
        ],
        2,
    )(grad_parts[0])

    part = columns // EXPERTS
    spec = pl.BlockSpec((rows, part), lambda e: (0, e))
    new_master, new_one, new_two, comb = pl.pallas_call(
        adam_kernel,
        grid=(EXPERTS,),
        out_shape=(
            shape((rows, columns), bf16),
            shape((rows, columns), f32),
            shape((rows, columns), f32),
            shape((Y, XZ, 128), f32),
        ),
        in_specs=[spec, spec, spec, spec, pl.BlockSpec((Y, 1, QBLOCK, tok), lambda e: (0, e, 0, 0))],
        out_specs=(spec, spec, spec, pl.BlockSpec((Y, XZ, 128), lambda e: (0, 0, 0))),
        scratch_shapes=[pltpu.VMEM((64, tok), f32)],
        compiler_params=pltpu.CompilerParams(vmem_limit_bytes=40 * 2**20),
    )(grad, master, moment_one, moment_two, hid_all)

    tile = pltpu.VMEM((8, 8, 128), f32)
    done = comm(
        deliver_kernel,
        shape((XZ, Y, 128), f32),
        [tile, tile, DMA((8,)), DMA((8,)), DMA((8,)), DMA((8,))],
        3,
    )(comb)
    done = done.reshape(XZ, Y, 2, 64)[..., :rows].transpose(2, 0, 1, 3).reshape(2, width)
    return new_master, new_one, new_two, done.astype(bf16)


def solution(mesh):
    in_specs = (
        P("wide", "narrow", None),
        P("narrow", None),
        P("narrow", None),
        P("narrow", None),
        P(None, None, "narrow"),
        P(("wide", "narrow"), None),
        P(("wide", "narrow"), None),
        P(("wide", "narrow"), None),
    )
    out_specs = (
        P("narrow", None),
        P("narrow", None),
        P("narrow", None),
        P(("wide", "narrow"), None),
    )
    return jax.shard_map(body, mesh=mesh, in_specs=in_specs, out_specs=out_specs, check_vma=False)
```

time: 1270 us -> 157 us (0.12)
  the two profiles are of different devices: /device:TPU:64 before, /device:TPU:8 now
where the time goes in v1:
time: 157 us
  Pallas kernels  151 us (96%)
  other arithmetic  2.3 us (1%)
  local copies, waits for them, and re-layouts  2.03 us (1%)
    pallas_call x1, Pallas kernels, body(): comm(hidden_kernel, shape((Y, XZ, QBLOCK, tok), bf16), GATHER_SEMS, 1)  44.7 us
    pallas_call x1, Pallas kernels, body(): comm(grads_kernel, shape((rows, columns), bf16), [pltpu.VMEM((rows, half)...  44.6 us
    pallas_call x1, Pallas kernels, body(): comm(tokens_kernel, shape((Y, 16, full), bf16), [pltpu.VMEM((XZ, 2, full)...  38.6 us
    pallas_call x1, Pallas kernels, body(): comm(deliver_kernel, shape((XZ, Y, 128), f32), [tile, tile, DMA((8,)), DM...  16.8 us
    pallas_call x1, Pallas kernels, body(): pl.pallas_call(adam_kernel, grid=(EXPERTS,), out_shape=(shape((rows, colu...  5.96 us

profile of v1, /device:TPU:8, one launch (start us, length us, event | category | flops | bytes accessed | tf_op | source)
XLA Modules:
  0.0 156.5 jit_solution(16166764428910506191)
XLA Ops:
  0.7 0.7 convert_element_type.21
  1.3 0.8 select_reduce_fusion.1
  2.1 0.7 fusion.6.own_ref
  2.8 0.0 copy-start.2
  2.8 1.2 copy-done.2
  4.0 0.0 copy-start.4
  4.0 44.6 %shard_map.111.g_ref = bf16[56,8192]{1,0:T(8,128)(2,1)S(1)} custom-call(bf16[56,8192]{1,0:T(8,128)(2,1)S(1)} %bitcast.14), custom_call_target="tpu_custom_call" | custom-call | tf_op jit(solution)/shard_map/pallas_call | solution.py:328
  48.6 38.6 %shard_map.112 = bf16[8,16,3712]{2,1,0:T(8,128)(2,1)S(1)} custom-call(bf16[2,3712]{1,0:T(2,128)(2,1)S(1)} %fusion.6.own_ref), custom_call_target="tpu_custom_call" | custom-call | tf_op jit(solution)/shard_map/pallas_call | solution.py:310
  87.2 0.1 select_reduce_fusion
  87.3 0.0 copy-done.4
  87.3 0.0 copy-start.1
  87.3 0.0 copy-start.3
  87.3 0.8 fusion
  88.2 0.0 copy-start
  88.2 44.7 %shard_map.113.hid_ref = bf16[8,8,128,128]{3,2,1,0:T(8,128)(2,1)S(1)} custom-call(bf16[128,128]{1,0:T(8,128)(2,1)S(1)} %fusion.5.own_ref), custom_call_target="tpu_custom_call" | custom-call | tf_op jit(solution)/shard_map/pallas_call | solution.py:324
  132.9 0.0 copy-done.1
  132.9 0.0 copy-done.3
  132.9 0.0 copy-done
  133.0 6.0 %shard_map.114 = (bf16[56,8192]{1,0:T(8,128)(2,1)}, f32[56,8192]{1,0:T(8,128)}, f32[56,8192]{1,0:T(8,128)}, f32[8,8,128]{2,1,0:T(8,128)S(1)}) custom-call(bf16[56,8192]{1,0:T(8,128)(2,1)S(1)} %shard_map.111.g_ref, bf16[56,8192]{1,0:T(8,128)(2,1)S(1)} %copy-done.3, f32[56,8192]{1,0:T(8,128)S(1)} %copy-done, f32[56,8192]{1,0:T(8,128)S(1)} %copy-done.1, ...), custom_call_target="tpu_custom_call" | custom-call | tf_op jit(solution)/shard_map/pallas_call | solution.py:342
  138.9 16.8 %shard_map.115 = f32[8,8,128]{2,1,0:T(8,128)S(1)} custom-call(f32[8,8,128]{2,1,0:T(8,128)S(1)} %get-tuple-element.11.comb_ref), custom_call_target="tpu_custom_call" | custom-call | tf_op jit(solution)/shard_map/pallas_call | solution.py:358
  155.7 0.1 reshape.29
  155.8 0.7 convert_element_type.26
  (5 shorter events, 0.1 us)
Async XLA Ops:
  2.8 1.2 copy-start.2
  4.0 83.3 %copy-start.4 = (bf16[3584,2,128]{2,1,0:T(2,128)(2,1)S(1)}, bf16[3584,2,128]{2,1,0:T(2,128)(2,1)}, u32[]{:S(2)}) copy-start(bf16[3584,2,128]{2,1,0:T(2,128)(2,1)} %param.12) | copy-start | bytes 5505028
  87.3 45.6 %copy-start.1 = (f32[56,8192]{1,0:T(8,128)S(1)}, f32[56,8192]{1,0:T(8,128)}, u32[]{:S(2)}) copy-start(f32[56,8192]{1,0:T(8,128)} %two_ref.1) | copy-start | bytes 5505028
  87.3 45.6 %copy-start.3 = (bf16[56,8192]{1,0:T(8,128)(2,1)S(1)}, bf16[56,8192]{1,0:T(8,128)(2,1)}, u32[]{:S(2)}) copy-start(bf16[56,8192]{1,0:T(8,128)(2,1)} %p_ref.1) | copy-start | bytes 2752516
  88.2 44.8 %copy-start = (f32[56,8192]{1,0:T(8,128)S(1)}, f32[56,8192]{1,0:T(8,128)}, u32[]{:S(2)}) copy-start(f32[56,8192]{1,0:T(8,128)} %one_ref.1) | copy-start | bytes 5505028

commit v2 on v0

v2 whole, which is shorter than its diff:
```python
import jax
import jax.numpy as jnp
from jax import lax
from jax.experimental import pallas as pl
from jax.experimental.pallas import tpu as pltpu
from jax.sharding import PartitionSpec as P

EXPERTS = 8
QBLOCK = 128
X, ZH, Y = 4, 2, 8
XZ = X * ZH
ZL = 6
CHUNKS = 8

beta_first = 0.9
beta_second = 0.95
learn_rate = 0.003
adam_eps = 1e-08
quant_limit = 448.0
amax_eps = 1e-06
bias_first = 1.0 - 0.9**10
bias_second = 1.0 - 0.95**10

VMEM = pl.BlockSpec(memory_space=pltpu.VMEM)
DMA = pltpu.SemaphoreType.DMA
f32 = jnp.float32
bf16 = jnp.bfloat16


def at_wide(index):
    return {"wide": index}


def remote(src, dst, send, recv, where):
    return pltpu.make_async_remote_copy(
        src_ref=src,
        dst_ref=dst,
        send_sem=send,
        recv_sem=recv,
        device_id=where,
        device_id_type=pl.DeviceIdType.MESH,
    )


def signal(where):
    pl.semaphore_signal(
        pltpu.get_barrier_semaphore(), inc=1, device_id=where, device_id_type=pl.DeviceIdType.MESH
    )


def place():
    n = lax.axis_index("narrow")
    return n // (ZH * Y), (n // Y) % ZH, n % Y


def device(x, zh, y):
    w = lax.axis_index("wide")
    own = (lax.axis_index("narrow") // Y) % ZH
    mirrored = (ZL - 1 - w // 2) * 2 + w % 2
    return {"wide": jnp.where(zh == own, w, mirrored), "narrow": (x * ZH + zh) * Y + y}


GATHER_SEMS = [DMA((9,))]
RING_SEMS = [DMA((4,)), DMA((4,)), DMA((4,)), DMA((4,))]


class Gather:
    def __init__(self, own, landing, sems):
        x, zh, y = place()
        me = x * ZH + zh
        self.local = pltpu.make_async_copy(own, landing.at[me], sems.at[8])
        self.cross = remote(own, landing.at[me], sems.at[0], sems.at[1], device(x, 1 - zh, y))
        pair = landing.at[pl.ds(x * ZH, ZH)]
        self.along = [
            remote(pair, pair, sems.at[1 + k], sems.at[4 + k], device((x + k) % X, zh, y))
            for k in range(1, X)
        ]

    def start(self):
        self.cross.start()
        self.local.start()

    def turn(self):
        self.local.wait()
        self.cross.wait()
        for copy in self.along:
            copy.start()

    def finish(self):
        for copy in self.along:
            copy.wait()


class Ring:
    def __init__(self, blocks, cut, right_send, right_recv, left_send, left_recv):
        x, zh, y = place()
        right, left = device(x, zh, (y + 1) % Y), device(x, zh, (y + Y - 1) % Y)
        self.steps = []
        for s in range(Y // 2):
            first, second = blocks.at[(y + Y - s) % Y], blocks.at[(y + s) % Y]
            if s == Y // 2 - 1:
                first, second = first.at[:, :cut], second.at[:, cut:]
            self.steps.append(
                (
                    remote(first, first, right_send.at[s], right_recv.at[s], right),
                    remote(second, second, left_send.at[s], left_recv.at[s], left),
                )
            )

    def start(self, s):
        for copy in self.steps[s]:
            copy.start()

    def wait(self, s):
        for copy in self.steps[s]:
            copy.wait()


class Sum:
    def __init__(self, g_ref, out_ref, pre, land, part, ps, pr, is_, ir, os_, or_, cs, cr):
        w = lax.axis_index("wide")
        zl, core = w // 2, w % 2
        half = g_ref.shape[1] // 2
        size = half // CHUNKS
        low = zl < ZL // 2
        edge = (zl == 0) | (zl == ZL - 1)
        mid = (zl == ZL // 2 - 1) | (zl == ZL // 2)
        inward = at_wide(jnp.where(low, w + 2, w - 2))
        outward = at_wide(jnp.where(edge, w, jnp.where(low, w - 2, w + 2)))
        other = at_wide(w + 1 - 2 * core)
        self.edge, self.mid, self.inner = edge, mid, jnp.logical_not(edge | mid)
        self.core, self.inward, self.outward, self.other = core, inward, outward, other
        self.g_ref, self.out_ref, self.pre, self.land, self.part = g_ref, out_ref, pre, land, part

        def span(core_of, k):
            return pl.ds(pl.multiple_of(core_of * half + k * size, size), size)

        def here(k):
            return pl.ds(k * size, size)

        def pre_copy(k):
            src = g_ref.at[:, span(1 - core, k)]
            return remote(src, pre.at[:, here(k)], ps.at[k], pr.at[k], other)

        def in_copy(k, slot):
            dst = land.at[slot, :, here(k)]
            return remote(part.at[:, here(k)], dst, is_.at[k], ir.at[slot, k], inward)

        def out_copy(k):
            cut = out_ref.at[:, span(core, k)]
            return remote(cut, cut, os_.at[k], or_.at[k], outward)

        def core_copy(k, which):
            cut = out_ref.at[:, span(which, k)]
            return remote(cut, cut, cs.at[k], cr.at[k], other)

        self.span, self.here = span, here
        self.pre_copy, self.in_copy, self.out_copy, self.core_copy = pre_copy, in_copy, out_copy, core_copy
        self.to_slot = jnp.where(mid, 1, 0)

    def greet(self):
        signal(self.inward)
        signal(self.other)
        pl.when(jnp.logical_not(self.edge))(lambda: signal(self.outward))
        return jnp.where(self.edge, 2, 3)

    def start(self):
        for k in range(CHUNKS):
            self.pre_copy(k).start()

    def inbound(self, k):
        self.pre_copy(k).wait_recv()
        here = self.here(k)
        total = self.g_ref[:, self.span(self.core, k)].astype(f32) + self.pre[:, here].astype(f32)

        @pl.when(self.edge)
        def _():
            self.part[:, here] = total.astype(bf16)

        @pl.when(jnp.logical_not(self.edge))
        def _():
            self.in_copy(k, 0).wait_recv()
            self.part[:, here] = (total + self.land[0, :, here].astype(f32)).astype(bf16)

        self.in_copy(k, self.to_slot).start()

    def outbound_mid(self, k):
        self.in_copy(k, 1).wait_recv()
        total = self.part[:, self.here(k)].astype(f32) + self.land[1, :, self.here(k)].astype(f32)
        self.out_ref[:, self.span(self.core, k)] = total.astype(bf16)
        self.out_copy(k).start()
        self.core_copy(k, self.core).start()

    def outbound_inner(self, k):
        self.out_copy(k).wait_recv()
        self.out_copy(k).start()
        self.core_copy(k, self.core).start()

    def outbound_edge(self, k):
        self.out_copy(k).wait_recv()
        self.core_copy(k, self.core).start()

    def step(self, s):
        if s < CHUNKS:
            self.inbound(s)
        for role, lag, run in (
            (self.mid, 1, self.outbound_mid),
            (self.inner, 3, self.outbound_inner),
            (self.edge, 5, self.outbound_edge),
        ):
            if 0 <= s - lag < CHUNKS:
                pl.when(role)(lambda run=run, k=s - lag: run(k))

    def finish(self):
        for k in range(CHUNKS):
            self.core_copy(k, 1 - self.core).wait_recv()
            self.pre_copy(k).wait_send()
            self.in_copy(k, self.to_slot).wait_send()
            self.core_copy(k, self.core).wait_send()

        @pl.when(jnp.logical_not(self.edge))
        def _():
            for k in range(CHUNKS):
                self.out_copy(k).wait_send()


def first_kernel(own_ref, g_ref, out_ref, sum_ref, landing, wide_rows, sems, rs, rr, ls, lr, *rest):
    x, zh, y = place()
    adding = Sum(g_ref, sum_ref, *rest)
    count = adding.greet()
    partners = [device(x, 1 - zh, y)]
    partners += [device((x + k) % X, zh, y) for k in range(1, X)]
    partners += [device(x, zh, (y + k) % Y) for k in (1, Y - 1)]
    for where in partners:
        signal(where)
    pl.semaphore_wait(pltpu.get_barrier_semaphore(), count + len(partners))

    gather = Gather(own_ref, landing, sems)
    width = own_ref.shape[1]
    ring = Ring(out_ref, width // 256 * 128, rs, rr, ls, lr)
    gather.start()
    adding.start()
    adding.step(0)
    adding.step(1)
    gather.turn()
    adding.step(2)
    adding.step(3)
    gather.finish()
    for j in range(XZ):
        for i in range(2):
            wide_rows[i * XZ + j : i * XZ + j + 1, :] = landing[j, i : i + 1, :].astype(f32)
    out_ref[pl.ds(y, 1)] = wide_rows[...].astype(bf16)[None]
    ring.start(0)
    for s in range(Y // 2):
        adding.step(4 + 2 * s)
        adding.step(5 + 2 * s)
        ring.wait(s)
        if s + 1 < Y // 2:
            ring.start(s + 1)
    for s in range(12, CHUNKS + 5):
        adding.step(s)
    adding.finish()


def adam_kernel(g_ref, p_ref, one_ref, two_ref, newp_ref, newone_ref, newtwo_ref, q_ref):
    step = pl.program_id(0)
    rows = g_ref.shape[0]
    half = EXPERTS // 2
    lane = lax.broadcasted_iota(jnp.int32, (rows, QBLOCK), 1)
    spot = step % half
    for b in range(Y):
        cut = slice(b * QBLOCK, (b + 1) * QBLOCK)
        grad = g_ref[:, cut].astype(f32)
        one = beta_first * one_ref[:, cut] + (1.0 - beta_first) * grad
        two = beta_second * two_ref[:, cut] + (1.0 - beta_second) * grad * grad
        newone_ref[:, cut] = one
        newtwo_ref[:, cut] = two
        step_dir = one * (1.0 / bias_first) / (jnp.sqrt(two * (1.0 / bias_second)) + adam_eps)
        updated = p_ref[:, cut].astype(f32) - learn_rate * step_dir
        newp_ref[:, cut] = updated.astype(bf16)
        amax = jnp.max(jnp.abs(updated), axis=1, keepdims=True)
        scale = ((amax + amax_eps) / quant_limit).astype(bf16).astype(f32)
        q_ref[0, b, :, pl.ds(pl.multiple_of(spot * QBLOCK, QBLOCK), QBLOCK)] = (
            updated * (1.0 / scale)
        ).astype(bf16)
        held = q_ref[0, b, :, half * QBLOCK :].astype(f32)
        held = jnp.where((spot == 0) | (lane > spot), 0.0, held)
        q_ref[0, b, :, half * QBLOCK :] = jnp.where(lane == spot, scale, held).astype(bf16)


def second_kernel(
    hid_ref, q_ref, out_ref, hid_all, rows_all, acc, sent, came, turned,
    sems, ys, yr, cs, cr, s1, r1, s2, r2,
):
    x, zh, y = place()
    w = lax.axis_index("wide")
    core = w % 2
    me = x * ZH + zh
    half = EXPERTS // 2
    rows = q_ref.shape[2]
    other = at_wide(w + 1 - 2 * core)
    column = [device(x, zh, (y + k) % Y) for k in range(1, Y)]
    plane = []
    for k in range(1, XZ):
        to = (me + k) % XZ
        plane.append(device(to // ZH, to % ZH, y))
    for where in column + plane + [other]:
        signal(where)
    pl.semaphore_wait(pltpu.get_barrier_semaphore(), len(column) + len(plane) + 1)

    gather = Gather(hid_ref, hid_all, sems)
    gather.start()
    relays = [
        remote(
            q_ref.at[core, (y + k) % Y], rows_all.at[core, y], ys.at[k], yr.at[k], column[k - 1]
        )
        for k in range(1, Y)
    ]
    order = [1, 7, 2, 6, 3, 5, 4]
    for k in order:
        relays[k - 1].start()
    mine = pltpu.make_async_copy(q_ref.at[core, y], rows_all.at[core, y], ys.at[0])
    mine.start()

    def share(k, which):
        part = rows_all.at[which, (y + Y - k) % Y]
        return remote(part, part, cs.at[k], cr.at[k], other)

    mine.wait()
    share(0, core).start()
    gather.turn()
    for k in order:
        relays[k - 1].wait_recv()
        share(k, core).start()
    gather.finish()

    def products(which, block):
        total = jnp.zeros((rows, hid_ref.shape[1]), f32)
        for e in range(half):
            quanta = rows_all[which, block, :, e * QBLOCK : (e + 1) * QBLOCK]
            scale = rows_all[which, block, :, half * QBLOCK + e : half * QBLOCK + e + 1].astype(f32)
            total += scale * jnp.dot(quanta, hid_all[which * half + e], preferred_element_type=f32)
        return total

    for j in range(Y):
        acc[j, :rows] = products(core, j)
    for k in [0] + order:
        share(k, 1 - core).wait_recv()
    for j in range(Y):
        acc[j, :rows] += products(1 - core, j)
        acc[j, rows:] = jnp.zeros_like(acc[j, rows:])
    for j in range(Y // 2):
        pair = jnp.concatenate([acc[2 * j], acc[2 * j + 1]], axis=0)
        pair = jnp.transpose(pair).astype(bf16)
        for t in range(Y):
            sent[t, :, j * QBLOCK : (j + 1) * QBLOCK] = pair[t * 16 : (t + 1) * 16]

    copies = []
    for k in order:
        to = (y + k) % Y
        copies.append(remote(sent.at[to], came.at[y], s1.at[k], r1.at[k], column[k - 1]))
        copies[-1].start()
    came[pl.ds(y, 1)] = sent[pl.ds(y, 1)]
    for copy in copies:
        copy.wait()
    total = came[0].astype(f32)
    for j in range(1, Y):
        total += came[j].astype(f32)
    for i in range(2):
        for q in range(4):
            turned[:, i * 4 + q, :] = total[i * 8 : (i + 1) * 8, q * 128 : (q + 1) * 128]
    copies = []
    for k in range(1, XZ):
        to = (me + k) % XZ
        copies.append(remote(turned.at[to], out_ref.at[me], s2.at[k], r2.at[k], plane[k - 1]))
        copies[-1].start()
    out_ref[pl.ds(me, 1)] = turned[pl.ds(me, 1)]
    for copy in copies:
        copy.wait()
    for k in order:
        relays[k - 1].wait_send()
    for k in range(Y):
        share(k, core).wait_send()


def comm(kernel, out_shape, scratch, number, inputs):
    return pl.pallas_call(
        kernel,
        out_shape=out_shape,
        in_specs=[VMEM] * inputs,
        out_specs=VMEM if not isinstance(out_shape, tuple) else (VMEM,) * len(out_shape),
        scratch_shapes=scratch,
        compiler_params=pltpu.CompilerParams(
            collective_id=number, has_side_effects=True, vmem_limit_bytes=40 * 2**20
        ),
    )


def body(grad_parts, master, moment_one, moment_two, gate_up, tokens, expert_ids, gate_vals):
    shape = jax.ShapeDtypeStruct
    rows, columns = master.shape
    width = tokens.shape[1]
    onehot = expert_ids[:, :, None] == jnp.arange(EXPERTS, dtype=jnp.int32)[None, None, :]
    weights = jnp.sum(jnp.where(onehot, gate_vals.astype(f32)[:, :, None], 0.0), axis=1).astype(bf16)
    packed = jnp.concatenate([tokens, jnp.pad(weights, ((0, 0), (0, QBLOCK - EXPERTS)))], axis=1)
    full = width + QBLOCK
    half = columns // 2
    sem = DMA((CHUNKS,))
    gathered, grad = comm(
        first_kernel,
        (shape((Y, 16, full), bf16), shape((rows, columns), bf16)),
        [pltpu.VMEM((XZ, 2, full), bf16), pltpu.VMEM((16, full), f32)]
        + GATHER_SEMS
        + RING_SEMS
        + [
            pltpu.VMEM((rows, half), bf16),
            pltpu.VMEM((2, rows, half), bf16),
            pltpu.VMEM((rows, half), bf16),
            sem, sem, sem, DMA((2, CHUNKS)), sem, sem, sem, sem,
        ],
        0,
        2,
    )(packed, grad_parts[0])
    gathered = gathered.reshape(Y * 16, full)

    proj = jnp.dot(gathered[:, :width], gate_up.reshape(width, 2 * QBLOCK), preferred_element_type=f32)
    expert = lax.axis_index("narrow") // Y
    chosen = jnp.arange(EXPERTS, dtype=jnp.int32) == expert
    weight = jnp.sum(jnp.where(chosen[None, :], gathered[:, width : width + EXPERTS].astype(f32), 0.0), axis=1)
    hidden = weight[:, None] * jax.nn.silu(proj[:, :QBLOCK]) * proj[:, QBLOCK:]
    hidden = hidden.astype(bf16).T
    tok = hidden.shape[1]

    part = columns // EXPERTS
    spec = pl.BlockSpec((rows, part), lambda e: (0, e))
    per = EXPERTS // 2
    lanes = (per + 1) * QBLOCK
    new_master, new_one, new_two, quanta = pl.pallas_call(
        adam_kernel,
        grid=(EXPERTS,),
        out_shape=(
            shape((rows, columns), bf16),
            shape((rows, columns), f32),
            shape((rows, columns), f32),
            shape((2, Y, rows, lanes), bf16),
        ),
        in_specs=[spec, spec, spec, spec],
        out_specs=(spec, spec, spec, pl.BlockSpec((1, Y, rows, lanes), lambda e: (e // per, 0, 0, 0))),
        compiler_params=pltpu.CompilerParams(vmem_limit_bytes=40 * 2**20),
    )(grad, master, moment_one, moment_two)

    sems = DMA((8,))
    done = comm(
        second_kernel,
        shape((XZ, Y, 128), f32),
        [
            pltpu.VMEM((XZ, QBLOCK, tok), bf16),
            pltpu.VMEM((2, Y, rows, lanes), bf16),
            pltpu.VMEM((Y, 64, tok), f32),
            pltpu.VMEM((Y, 16, 512), bf16),
            pltpu.VMEM((Y, 16, 512), bf16),
            pltpu.VMEM((XZ, 8, 128), f32),
        ]
        + GATHER_SEMS
        + [sems] * 8,
        1,
        2,
    )(hidden, quanta)
    done = done.reshape(XZ, 2, Y, 64)[..., :rows].transpose(1, 0, 2, 3).reshape(2, width)
    return new_master, new_one, new_two, done.astype(bf16)


def solution(mesh):
    in_specs = (
        P("wide", "narrow", None),
        P("narrow", None),
        P("narrow", None),
        P("narrow", None),
        P(None, None, "narrow"),
        P(("wide", "narrow"), None),
        P(("wide", "narrow"), None),
        P(("wide", "narrow"), None),
    )
    out_specs = (
        P("narrow", None),
        P("narrow", None),
        P("narrow", None),
        P(("wide", "narrow"), None),
    )
    return jax.shard_map(body, mesh=mesh, in_specs=in_specs, out_specs=out_specs, check_vma=False)
```

time: 1270 us -> 102 us (0.08)
  the two profiles are of different devices: /device:TPU:64 before, /device:TPU:1 now
where the time goes in v2:
time: 102 us; the launch traced here: 101 us
  Pallas kernels  92.7 us (91%)
  local copies, waits for them, and re-layouts  3.17 us (3%)
  matrix products  2.44 us (2%)
  other arithmetic  2.3 us (2%)
    pallas_call x1, Pallas kernels, body(): comm(first_kernel, (shape((Y, 16, full), bf16), shape((rows, columns), bf...  53.1 us
    pallas_call x1, Pallas kernels, body(): comm(second_kernel, shape((XZ, Y, 128), f32), [pltpu.VMEM((XZ, QBLOCK, to...  34.9 us
    pallas_call x1, Pallas kernels, body(): pl.pallas_call(adam_kernel, grid=(EXPERTS,), out_shape=(shape((rows, colu...  4.66 us
    dot_general x1, matrix products, body(): jnp.dot(gathered[:, :width], gate_up.reshape(width, 2 * QBLOCK), preferre...  2.44 us
    unnamed x8, local copies, waits for them, and re-layouts  2.36 us

profile of v2, /device:TPU:1, one launch (start us, length us, event | category | flops | bytes accessed | tf_op | source)
XLA Modules:
  0.0 101.3 jit_solution(709312855622048770)
XLA Ops:
  0.7 0.7 convert_element_type.21
  1.3 0.8 select_reduce_fusion.1
  2.1 0.7 fusion.6.own_ref
  2.8 0.0 copy-start.2
  2.8 1.2 %copy-done.2 = bf16[1,56,8192]{2,1,0:T(8,128)(2,1)S(1)} copy-done((bf16[1,56,8192]{2,1,0:T(8,128)(2,1)S(1)}, bf16[1,56,8192]{2,1,0:T(8,128)(2,1)}, u32[]{:S(2)}) %copy-start.2) | copy-done | bytes 917528
  4.0 0.0 copy-start.1
  4.0 53.1 %shard_map.111 = (bf16[8,16,3712]{2,1,0:T(8,128)(2,1)S(1)}, bf16[56,8192]{1,0:T(8,128)(2,1)S(1)}) custom-call(bf16[2,3712]{1,0:T(2,128)(2,1)S(1)} %fusion.6.own_ref, bf16[56,8192]{1,0:T(8,128)(2,1)S(1)} %bitcast.12), custom_call_target="tpu_custom_call" | custom-call | tf_op jit(solution)/shard_map/pallas_call | solution.py:409
  57.1 0.0 copy-start
  57.1 0.1 select_reduce_fusion
  57.2 2.4 %fusion = f32[128,256]{0,1:T(8,128)S(1)} fusion(bf16[448,8,2,128]{3,2,1,0:T(2,128)(2,1)} %bitcast.15, bf16[128,3712]{1,0:T(8,128)(2,1)S(1)} %bitcast.14), kind=kOutput, calls=%fused_computation | convolution fusion | flops 234881024 | bytes 2883584 | tf_op jit(solution)/shard_map/dot_general | solution.py:426
  59.7 0.0 copy-done.1
  59.7 0.0 copy-done
  59.7 0.0 copy-start.3
  59.7 1.2 %copy-done.3 = bf16[56,8192]{1,0:T(8,128)(2,1)S(1)} copy-done((bf16[56,8192]{1,0:T(8,128)(2,1)S(1)}, bf16[56,8192]{1,0:T(8,128)(2,1)}, u32[]{:S(2)}) %copy-start.3) | copy-done | bytes 917528
  60.9 4.7 %shard_map.112 = (bf16[56,8192]{1,0:T(8,128)(2,1)}, f32[56,8192]{1,0:T(8,128)}, f32[56,8192]{1,0:T(8,128)}, bf16[2,8,56,640]{3,2,1,0:T(8,128)(2,1)S(1)}) custom-call(bf16[56,8192]{1,0:T(8,128)(2,1)S(1)} %get-tuple-element.10.g_ref, bf16[56,8192]{1,0:T(8,128)(2,1)S(1)} %copy-done.3, f32[56,8192]{1,0:T(8,128)S(1)} %copy-done, f32[56,8192]{1,0:T(8,128)S(1)} %copy-done.1), custom_call_target="tpu_custom_call" | custom-call | tf_op jit(solution)/shard_map/pallas_call | solution.py:438
  65.6 34.9 %shard_map.113 = f32[8,8,128]{2,1,0:T(8,128)S(1)} custom-call(bf16[128,128]{1,0:T(8,128)(2,1)S(1)} %fusion.5.hid_ref, bf16[2,8,56,640]{3,2,1,0:T(8,128)(2,1)S(1)} %get-tuple-element.15.q_ref), custom_call_target="tpu_custom_call" | custom-call | tf_op jit(solution)/shard_map/pallas_call | solution.py:453
  100.5 0.1 reshape.29
  100.6 0.7 convert_element_type.26
  (5 shorter events, 0.1 us)
Async XLA Ops:
  2.8 1.2 %copy-start.2 = (bf16[1,56,8192]{2,1,0:T(8,128)(2,1)S(1)}, bf16[1,56,8192]{2,1,0:T(8,128)(2,1)}, u32[]{:S(2)}) copy-start(bf16[1,56,8192]{2,1,0:T(8,128)(2,1)} %param.8) | copy-start | bytes 2752516
  4.0 55.7 %copy-start.1 = (f32[56,8192]{1,0:T(8,128)S(1)}, f32[56,8192]{1,0:T(8,128)}, u32[]{:S(2)}) copy-start(f32[56,8192]{1,0:T(8,128)} %two_ref.1) | copy-start | bytes 5505028
  57.1 2.6 %copy-start = (f32[56,8192]{1,0:T(8,128)S(1)}, f32[56,8192]{1,0:T(8,128)}, u32[]{:S(2)}) copy-start(f32[56,8192]{1,0:T(8,128)} %one_ref.1) | copy-start | bytes 5505028
  59.7 1.2 %copy-start.3 = (bf16[56,8192]{1,0:T(8,128)(2,1)S(1)}, bf16[56,8192]{1,0:T(8,128)(2,1)}, u32[]{:S(2)}) copy-start(bf16[56,8192]{1,0:T(8,128)(2,1)} %p_ref.1) | copy-start | bytes 2752516

commit v3 on v2

v3 whole, which is shorter than its diff:
```python
import jax
import jax.numpy as jnp
from jax import lax
from jax.experimental import pallas as pl
from jax.experimental.pallas import tpu as pltpu
from jax.sharding import PartitionSpec as P

EXPERTS = 8
QBLOCK = 128
X, ZH, Y = 4, 2, 8
XZ = X * ZH
ZL = 6
CHUNKS = 4

beta_first = 0.9
beta_second = 0.95
learn_rate = 0.003
adam_eps = 1e-08
quant_limit = 448.0
amax_eps = 1e-06
bias_first = 1.0 - 0.9**10
bias_second = 1.0 - 0.95**10

VMEM = pl.BlockSpec(memory_space=pltpu.VMEM)
ANY = pl.BlockSpec(memory_space=pl.ANY)
DMA = pltpu.SemaphoreType.DMA
f32 = jnp.float32
bf16 = jnp.bfloat16


def at_wide(index):
    return {"wide": index}


def remote(src, dst, send, recv, where):
    return pltpu.make_async_remote_copy(
        src_ref=src,
        dst_ref=dst,
        send_sem=send,
        recv_sem=recv,
        device_id=where,
        device_id_type=pl.DeviceIdType.MESH,
    )


def signal(where):
    pl.semaphore_signal(
        pltpu.get_barrier_semaphore(), inc=1, device_id=where, device_id_type=pl.DeviceIdType.MESH
    )


def place():
    n = lax.axis_index("narrow")
    return n // (ZH * Y), (n // Y) % ZH, n % Y


def device(x, zh, y):
    w = lax.axis_index("wide")
    own = (lax.axis_index("narrow") // Y) % ZH
    mirrored = (ZL - 1 - w // 2) * 2 + w % 2
    return {"wide": jnp.where(zh == own, w, mirrored), "narrow": (x * ZH + zh) * Y + y}


GATHER_SEMS = [DMA((9,))]
RING_SEMS = [DMA((4,)), DMA((4,)), DMA((4,)), DMA((4,))]


class Gather:
    def __init__(self, own, landing, sems):
        x, zh, y = place()
        me = x * ZH + zh
        self.local = pltpu.make_async_copy(own, landing.at[me], sems.at[8])
        self.cross = remote(own, landing.at[me], sems.at[0], sems.at[1], device(x, 1 - zh, y))
        pair = landing.at[pl.ds(x * ZH, ZH)]
        self.along = [
            remote(pair, pair, sems.at[1 + k], sems.at[4 + k], device((x + k) % X, zh, y))
            for k in range(1, X)
        ]

    def start(self):
        self.cross.start()
        self.local.start()

    def turn(self):
        self.local.wait()
        self.cross.wait()
        for copy in self.along:
            copy.start()

    def finish(self):
        for copy in self.along:
            copy.wait()


class Ring:
    def __init__(self, blocks, cut, right_send, right_recv, left_send, left_recv):
        x, zh, y = place()
        right, left = device(x, zh, (y + 1) % Y), device(x, zh, (y + Y - 1) % Y)
        self.steps = []
        for s in range(Y // 2):
            first, second = blocks.at[(y + Y - s) % Y], blocks.at[(y + s) % Y]
            if s == Y // 2 - 1:
                first, second = first.at[:, :cut], second.at[:, cut:]
            self.steps.append(
                (
                    remote(first, first, right_send.at[s], right_recv.at[s], right),
                    remote(second, second, left_send.at[s], left_recv.at[s], left),
                )
            )

    def start(self, s):
        for copy in self.steps[s]:
            copy.start()

    def wait(self, s):
        for copy in self.steps[s]:
            copy.wait()


class Sum:
    def __init__(self, g_ref, out_ref, own, pre, land, part, ld, ps, pr, is_, ir, os_, or_, cs, cr):
        w = lax.axis_index("wide")
        zl, core = w // 2, w % 2
        half = g_ref.shape[1] // 2
        size = half // CHUNKS
        low = zl < ZL // 2
        edge = (zl == 0) | (zl == ZL - 1)
        mid = (zl == ZL // 2 - 1) | (zl == ZL // 2)
        inward = at_wide(jnp.where(low, w + 2, w - 2))
        outward = at_wide(jnp.where(edge, w, jnp.where(low, w - 2, w + 2)))
        other = at_wide(w + 1 - 2 * core)
        self.edge, self.mid, self.inner = edge, mid, jnp.logical_not(edge | mid)
        self.core, self.inward, self.outward, self.other = core, inward, outward, other
        self.out_ref, self.own, self.pre, self.land, self.part = out_ref, own, pre, land, part
        self.to_slot = jnp.where(mid, 1, 0)

        def span(core_of, k):
            return pl.ds(pl.multiple_of(core_of * half + k * size, size), size)

        def load(k):
            return pltpu.make_async_copy(g_ref.at[:, span(core, k)], own.at[k], ld.at[k])

        def pre_copy(k):
            return remote(g_ref.at[:, span(1 - core, k)], pre.at[k], ps.at[k], pr.at[k], other)

        def in_copy(k, slot):
            return remote(part.at[k], land.at[slot, k], is_.at[k], ir.at[slot, k], inward)

        def out_copy(k):
            cut = out_ref.at[core, k]
            return remote(cut, cut, os_.at[k], or_.at[k], outward)

        def core_copy(k, which):
            cut = out_ref.at[which, k]
            return remote(cut, cut, cs.at[k], cr.at[k], other)

        self.load, self.pre_copy, self.in_copy, self.out_copy, self.core_copy = (
            load, pre_copy, in_copy, out_copy, core_copy,
        )

    def greet(self):
        signal(self.inward)
        signal(self.other)
        pl.when(jnp.logical_not(self.edge))(lambda: signal(self.outward))
        return jnp.where(self.edge, 2, 3)

    def start(self):
        for k in range(CHUNKS):
            self.pre_copy(k).start()

    def inbound(self, k):
        self.load(k).wait()
        self.pre_copy(k).wait_recv()

        @pl.when(self.edge)
        def _():
            self.part[k] = (self.own[k].astype(f32) + self.pre[k].astype(f32)).astype(bf16)

        @pl.when(jnp.logical_not(self.edge))
        def _():
            self.in_copy(k, 0).wait_recv()
            total = self.own[k].astype(f32) + self.pre[k].astype(f32)
            self.part[k] = (total + self.land[0, k].astype(f32)).astype(bf16)

        self.in_copy(k, self.to_slot).start()

    def middle(self, k):
        @pl.when(self.mid)
        def _():
            self.in_copy(k, 1).wait_recv()
            total = self.part[k].astype(f32) + self.land[1, k].astype(f32)
            self.out_ref[pl.ds(self.core, 1), k] = total.astype(bf16)[None]
            self.out_copy(k).start()
            self.core_copy(k, self.core).start()

    def inner_out(self, k):
        @pl.when(self.inner)
        def _():
            self.out_copy(k).wait_recv()
            self.out_copy(k).start()
            self.core_copy(k, self.core).start()

    def edge_out(self, k):
        @pl.when(self.edge)
        def _():
            self.out_copy(k).wait_recv()
            self.core_copy(k, self.core).start()

    def finish(self):
        for k in range(CHUNKS):
            self.core_copy(k, 1 - self.core).wait_recv()
            self.pre_copy(k).wait_send()
            self.in_copy(k, self.to_slot).wait_send()
            self.core_copy(k, self.core).wait_send()

        @pl.when(jnp.logical_not(self.edge))
        def _():
            for k in range(CHUNKS):
                self.out_copy(k).wait_send()


def adam(grad, master, moment_one, moment_two):
    one = beta_first * moment_one + (1.0 - beta_first) * grad
    two = beta_second * moment_two + (1.0 - beta_second) * grad * grad
    step_dir = one * (1.0 / bias_first) / (jnp.sqrt(two * (1.0 / bias_second)) + adam_eps)
    return one, two, master - learn_rate * step_dir


def main_kernel(
    tok_ref, ids_ref, gate_ref, g_ref, p_ref, one_ref, two_ref, w_ref,
    sum_ref, out_ref,
    own, landing, wide_rows, gathered, w_raw, w_tmp, w_both,
    p_half, one_half, two_half, q_send, rows_all, hid_own, hid_all, acc, sent, came, turned, both,
    ld, sems, rs, rr, ls, lr, hsems, ys, yr, cs, cr, s1, r1, s2, r2, *rest
):
    x, zh, y = place()
    w = lax.axis_index("wide")
    core = w % 2
    other = at_wide(w + 1 - 2 * core)
    expert = x * ZH + zh
    rows, columns = p_ref.shape
    half = columns // 2
    width = tok_ref.shape[1]
    per = EXPERTS // 2
    batches, fit = 2, per // 2
    adding = Sum(g_ref, sum_ref, *rest)

    count = adding.greet()
    column = [device(x, zh, (y + k) % Y) for k in range(1, Y)]
    near = [device(x, 1 - zh, y)] + [device((x + k) % X, zh, y) for k in range(1, X)]
    for where in column + near:
        signal(where)

    span = pl.ds(pl.multiple_of(core * half, half), half)
    w_load = pltpu.make_async_copy(w_ref, w_raw, ld.at[0])
    state_loads = [
        pltpu.make_async_copy(p_ref.at[:, span], p_half, ld.at[1]),
        pltpu.make_async_copy(one_ref.at[:, span], one_half, ld.at[2]),
        pltpu.make_async_copy(two_ref.at[:, span], two_half, ld.at[3]),
    ]
    for k in range(CHUNKS):
        adding.load(k).start()
    w_load.start()
    for copy in state_loads:
        copy.start()

    own[:, :width] = tok_ref[...]
    lane = lax.broadcasted_iota(jnp.int32, (2, QBLOCK), 1)
    weights = jnp.zeros((2, QBLOCK), f32)
    for k in range(ids_ref.shape[1]):
        gate = gate_ref[:, k : k + 1].astype(f32)
        weights += jnp.where(ids_ref[:, k : k + 1] == lane, gate, 0.0)
    own[:, width:] = weights.astype(bf16)
    pl.semaphore_wait(pltpu.get_barrier_semaphore(), count + len(column) + len(near))

    gather = Gather(own, landing, sems)
    ring = Ring(gathered, own.shape[1] // 256 * 128, rs, rr, ls, lr)
    gather.start()
    adding.start()

    w_load.wait()
    piece = w_tmp.shape[0]

    def split(i, carry):
        w_tmp[...] = w_raw[pl.ds(pl.multiple_of(i * piece, piece), piece), :].astype(f32)
        to = pl.ds(pl.multiple_of(i * (piece // 2), piece // 2), piece // 2)
        w_both[to, :QBLOCK] = w_tmp[pl.ds(0, piece // 2, stride=2), :].astype(bf16)
        w_both[to, QBLOCK:] = w_tmp[pl.ds(1, piece // 2, stride=2), :].astype(bf16)
        return carry

    lax.fori_loop(0, w_raw.shape[0] // piece, split, 0)

    gather.turn()
    adding.inbound(0)
    gather.finish()
    for j in range(XZ):
        for i in range(2):
            wide_rows[i * XZ + j : i * XZ + j + 1, :] = landing[j, i : i + 1, :].astype(f32)
    gathered[pl.ds(y, 1)] = wide_rows[...].astype(bf16)[None]
    ring.start(0)
    for copy in state_loads:
        copy.wait()

    def quantize(k):
        batch, spot = k // fit, k % fit
        for b in range(Y):
            cut = slice(k * Y * QBLOCK + b * QBLOCK, k * Y * QBLOCK + (b + 1) * QBLOCK)
            grad = sum_ref[core, k, :, b * QBLOCK : (b + 1) * QBLOCK].astype(f32)
            _, _, updated = adam(grad, p_half[:, cut].astype(f32), one_half[:, cut], two_half[:, cut])
            amax = jnp.max(jnp.abs(updated), axis=1, keepdims=True)
            scale = ((amax + amax_eps) / quant_limit).astype(bf16)
            quanta = (updated * (1.0 / scale.astype(f32))).astype(bf16)
            q_send[batch, b, :, spot * QBLOCK : (spot + 1) * QBLOCK] = quanta
            q_send[batch, b, :, fit * QBLOCK + spot : fit * QBLOCK + spot + 1] = scale

    order = [1, 7, 2, 6, 3, 5, 4]

    def relay(batch, k):
        return remote(
            q_send.at[batch, (y + k) % Y], rows_all.at[core, batch, y],
            ys.at[batch, k], yr.at[batch, k], column[k - 1],
        )

    def mine(batch):
        return pltpu.make_async_copy(
            q_send.at[batch, y], rows_all.at[core, batch, y], ys.at[batch, 0]
        )

    def relay_start(batch):
        for k in order:
            relay(batch, k).start()
        mine(batch).start()

    def share(batch, which):
        part = rows_all.at[which, batch]
        return remote(part, part, cs.at[batch], cr.at[batch], other)

    def relay_finish(batch):
        mine(batch).wait()
        for k in order:
            relay(batch, k).wait_recv()
        share(batch, core).start()

    adding.inbound(1)
    adding.inbound(2)
    adding.middle(0)
    ring.wait(0)
    ring.start(1)
    adding.inbound(3)
    adding.middle(1)
    adding.middle(2)
    adding.inner_out(0)
    ring.wait(1)
    ring.start(2)
    adding.middle(3)
    adding.inner_out(1)
    adding.inner_out(2)
    adding.edge_out(0)
    ring.wait(2)
    ring.start(3)
    quantize(0)
    adding.inner_out(3)
    adding.edge_out(1)
    quantize(1)
    relay_start(0)
    adding.edge_out(2)
    ring.wait(3)

    tokens = gathered.reshape(Y * 16, own.shape[1])
    proj = jnp.dot(tokens[:, :width], w_both[...], preferred_element_type=f32)
    weight = tokens[:, width:].astype(f32)
    lanes = lax.broadcasted_iota(jnp.int32, weight.shape, 1)
    weight = jnp.sum(jnp.where(lanes == expert, weight, 0.0), axis=1, keepdims=True)
    gate = proj[:, :QBLOCK]
    hidden = weight * (gate * jax.nn.sigmoid(gate)) * proj[:, QBLOCK:]
    hid_own[...] = jnp.transpose(hidden).astype(bf16)
    hid_gather = Gather(hid_own, hid_all, hsems)
    hid_gather.start()
    adding.edge_out(3)
    quantize(2)
    quantize(3)
    relay_start(1)
    relay_finish(0)
    hid_gather.turn()
    relay_finish(1)
    hid_gather.finish()

    def products(which, batch):
        for j in range(Y):
            total = None
            for e in range(fit):
                quanta = rows_all[which, batch, j, :, e * QBLOCK : (e + 1) * QBLOCK]
                scale = rows_all[which, batch, j, :, fit * QBLOCK + e : fit * QBLOCK + e + 1]
                term = scale.astype(f32) * jnp.dot(
                    quanta, hid_all[which * per + batch * fit + e], preferred_element_type=f32
                )
                total = term if total is None else total + term
            yield j, total

    for j, total in products(core, 0):
        acc[j, :rows] = total
        acc[j, rows:] = jnp.zeros_like(acc[j, rows:])
    for j, total in products(core, 1):
        acc[j, :rows] += total
    for batch in range(batches):
        share(batch, 1 - core).wait_recv()
        for j, total in products(1 - core, batch):
            acc[j, :rows] += total

    for j in range(Y // 2):
        pair = jnp.concatenate([acc[2 * j], acc[2 * j + 1]], axis=0)
        pair = jnp.transpose(pair).astype(bf16)
        for t in range(Y):
            sent[t, :, j * QBLOCK : (j + 1) * QBLOCK] = pair[t * 16 : (t + 1) * 16]
    copies = []
    for k in order:
        to = (y + k) % Y
        copies.append(remote(sent.at[to], came.at[y], s1.at[k], r1.at[k], column[k - 1]))
        copies[-1].start()
    came[pl.ds(y, 1)] = sent[pl.ds(y, 1)]
    for copy in copies:
        copy.wait()
    total = came[0].astype(f32)
    for j in range(1, Y):
        total += came[j].astype(f32)
    for i in range(2):
        for q in range(4):
            part = total[i * 8 : (i + 1) * 8, q * 128 : (q + 1) * 128]
            for j in range(XZ):
                turned[j % ZH, j // ZH, i * 4 + q : i * 4 + q + 1, :] = part[j : j + 1]
    cross = remote(turned.at[1 - zh], both.at[zh], s2.at[0], r2.at[0], near[0])
    cross.start()
    both[pl.ds(zh, 1)] = turned[pl.ds(zh, 1)]
    cross.wait()
    copies = []
    for k in range(1, X):
        src = both.at[:, (x + k) % X]
        copies.append(remote(src, out_ref.at[:, x], s2.at[k], r2.at[k], near[k]))
        copies[-1].start()
    for i in range(ZH):
        out_ref[i, pl.ds(x, 1)] = both[i, pl.ds(x, 1)]
    for copy in copies:
        copy.wait()

    for batch in range(batches):
        for k in order:
            relay(batch, k).wait_send()
        share(batch, core).wait_send()
    adding.finish()


def adam_kernel(g_ref, p_ref, one_ref, two_ref, newp_ref, newone_ref, newtwo_ref):
    for b in range(g_ref.shape[3] // QBLOCK):
        cut = slice(b * QBLOCK, (b + 1) * QBLOCK)
        one, two, updated = adam(
            g_ref[0, 0, :, cut].astype(f32), p_ref[:, cut].astype(f32), one_ref[:, cut], two_ref[:, cut]
        )
        newone_ref[:, cut] = one
        newtwo_ref[:, cut] = two
        newp_ref[:, cut] = updated.astype(bf16)


def body(grad_parts, master, moment_one, moment_two, gate_up, tokens, expert_ids, gate_vals):
    shape = jax.ShapeDtypeStruct
    rows, columns = master.shape
    width = tokens.shape[1]
    full = width + QBLOCK
    half = columns // 2
    size = half // CHUNKS
    tok = Y * 16
    sem = DMA((CHUNKS,))
    chunk = pltpu.VMEM((CHUNKS, rows, size), bf16)
    total, done = pl.pallas_call(
        main_kernel,
        out_shape=(
            shape((2, CHUNKS, rows, size), bf16),
            shape((ZH, X, 8, 128), f32),
        ),
        in_specs=[VMEM] * 3 + [ANY] * 5,
        out_specs=(VMEM, VMEM),
        scratch_shapes=[
            pltpu.VMEM((2, full), bf16),
            pltpu.VMEM((XZ, 2, full), bf16),
            pltpu.VMEM((16, full), f32),
            pltpu.VMEM((Y, 16, full), bf16),
            pltpu.VMEM((2 * width, QBLOCK), bf16),
            pltpu.VMEM((512, QBLOCK), f32),
            pltpu.VMEM((width, 2 * QBLOCK), bf16),
            pltpu.VMEM((rows, half), bf16),
            pltpu.VMEM((rows, half), f32),
            pltpu.VMEM((rows, half), f32),
            pltpu.VMEM((2, Y, rows, 3 * QBLOCK), bf16),
            pltpu.VMEM((2, 2, Y, rows, 3 * QBLOCK), bf16),
            pltpu.VMEM((QBLOCK, tok), bf16),
            pltpu.VMEM((XZ, QBLOCK, tok), bf16),
            pltpu.VMEM((Y, 64, tok), f32),
            pltpu.VMEM((Y, 16, 512), bf16),
            pltpu.VMEM((Y, 16, 512), bf16),
            pltpu.VMEM((ZH, X, 8, 128), f32),
            pltpu.VMEM((ZH, X, 8, 128), f32),
            DMA((4,)),
        ]
        + GATHER_SEMS
        + RING_SEMS
        + GATHER_SEMS
        + [DMA((2, 8)), DMA((2, 8)), DMA((2,)), DMA((2,)), DMA((8,)), DMA((8,)), DMA((4,)), DMA((4,))]
        + [chunk, chunk, pltpu.VMEM((2, CHUNKS, rows, size), bf16), chunk]
        + [sem, sem, sem, sem, DMA((2, CHUNKS)), sem, sem, sem, sem],
        compiler_params=pltpu.CompilerParams(
            collective_id=0, has_side_effects=True, vmem_limit_bytes=48 * 2**20
        ),
    )(
        tokens, expert_ids, gate_vals, grad_parts[0], master, moment_one, moment_two,
        gate_up.reshape(2 * width, QBLOCK),
    )

    spec = pl.BlockSpec((rows, size), lambda e: (0, e))
    new_master, new_one, new_two = pl.pallas_call(
        adam_kernel,
        grid=(2 * CHUNKS,),
        out_shape=(
            shape((rows, columns), bf16),
            shape((rows, columns), f32),
            shape((rows, columns), f32),
        ),
        in_specs=[pl.BlockSpec((1, 1, rows, size), lambda e: (e // CHUNKS, e % CHUNKS, 0, 0)), spec, spec, spec],
        out_specs=(spec, spec, spec),
        compiler_params=pltpu.CompilerParams(vmem_limit_bytes=40 * 2**20),
    )(total, master, moment_one, moment_two)

    done = done.reshape(ZH, X, 2, Y, 64)[..., :rows].transpose(2, 1, 0, 3, 4).reshape(2, width)
    return new_master, new_one, new_two, done.astype(bf16)


def solution(mesh):
    in_specs = (
        P("wide", "narrow", None),
        P("narrow", None),
        P("narrow", None),
        P("narrow", None),
        P(None, None, "narrow"),
        P(("wide", "narrow"), None),
        P(("wide", "narrow"), None),
        P(("wide", "narrow"), None),
    )
    out_specs = (
        P("narrow", None),
        P("narrow", None),
        P("narrow", None),
        P(("wide", "narrow"), None),
    )
    return jax.shard_map(body, mesh=mesh, in_specs=in_specs, out_specs=out_specs, check_vma=False)
```

time: 102 us -> 95.5 us (0.936)
  the two profiles are of different devices: /device:TPU:1 before, /device:TPU:128 now
where the time goes in v3:
time: 95.5 us; the launch traced here: 95.1 us
  Pallas kernels  84.1 us (88%)
  local copies, waits for them, and re-layouts  10.3 us (11%)
    pallas_call x1, Pallas kernels, body(): pl.pallas_call(main_kernel, out_shape=(shape((2, CHUNKS, rows, size), bf1...  80 us
    unnamed x22, local copies, waits for them, and re-layouts  9.5 us
    pallas_call x1, Pallas kernels, body(): pl.pallas_call(adam_kernel, grid=(2 * CHUNKS,), out_shape=(shape((rows, c...  4.12 us

profile of v3, /device:TPU:128, one launch (start us, length us, event | category | flops | bytes accessed | tf_op | source)
XLA Modules:
  0.0 95.1 jit_solution(7272577606390155029)
XLA Ops:
  0.6 0.0 copy-start
  0.6 1.5 %copy-done = f32[56,8192]{1,0:T(8,128)S(1)} copy-done((f32[56,8192]{1,0:T(8,128)S(1)}, f32[56,8192]{1,0:T(8,128)}, u32[]{:S(2)}) %copy-start) | copy-done | bytes 1835032
  2.1 0.0 copy-start.3
  2.1 1.2 %copy-done.3 = bf16[56,8192]{1,0:T(8,128)(2,1)S(1)} copy-done((bf16[56,8192]{1,0:T(8,128)(2,1)S(1)}, bf16[56,8192]{1,0:T(8,128)(2,1)}, u32[]{:S(2)}) %copy-start.3) | copy-done | bytes 917528
  3.3 0.0 copy-start.5
  3.3 1.2 %copy-done.5 = bf16[1,56,8192]{2,1,0:T(8,128)(2,1)S(1)} copy-done((bf16[1,56,8192]{2,1,0:T(8,128)(2,1)S(1)}, bf16[1,56,8192]{2,1,0:T(8,128)(2,1)}, u32[]{:S(2)}) %copy-start.5) | copy-done | bytes 917528
  4.5 0.0 copy-start.8
  4.5 0.7 copy-done.8
  5.2 0.0 copy-start.9
  5.2 0.7 copy-done.9
  5.9 0.0 copy-start.10
  5.9 0.7 copy-done.10
  6.5 0.0 copy-start.1
  6.5 0.0 copy-start.4
  6.5 80.0 %shard_map.111 = (bf16[2,4,56,1024]{3,2,1,0:T(8,128)(2,1)S(1)}, f32[2,4,8,128]{3,2,1,0:T(8,128)S(1)}) custom-call(bf16[2,3584]{1,0:T(2,128)(2,1)S(1)} %copy-done.8, s32[2,4]{1,0:T(2,128)S(1)} %copy-done.9, bf16[2,4]{1,0:T(2,128)(2,1)S(1)} %copy-done.10, bf16[56,8192]{1,0:T(8,128)(2,1)S(1)} %bitcast.8, bf16[56,8192]{1,0:T(8,128)(2,1)S(1)} %copy-done.3, ...), custom_call_target="tpu_custom_call" | custom-call | tf_op jit(solution)/shard_map/pallas_call | solution.py:473
  86.5 0.0 copy-start.6
  86.5 0.9 copy-done.6
  87.5 0.1 reshape.18
  87.6 0.7 convert_element_type.8
  88.3 0.0 copy-done.1
  88.3 0.0 copy-done.4
  88.3 0.0 copy-start.2
  88.3 1.5 %copy-done.2 = f32[56,8192]{1,0:T(8,128)S(1)} copy-done((f32[56,8192]{1,0:T(8,128)S(1)}, f32[56,8192]{1,0:T(8,128)}, u32[]{:S(2)}) %copy-start.2) | copy-done | bytes 1835032
  89.8 0.0 copy-start.7
  89.8 1.2 %copy-done.7 = bf16[2,4,56,1024]{3,2,1,0:T(8,128)(2,1)S(1)} copy-done((bf16[2,4,56,1024]{3,2,1,0:T(8,128)(2,1)S(1)}, bf16[2,4,56,1024]{3,2,1,0:T(8,128)(2,1)}, u32[]{:S(2)}) %copy-start.7) | copy-done | bytes 917528
  91.0 4.1 %shard_map.112 = (bf16[56,8192]{1,0:T(8,128)(2,1)}, f32[56,8192]{1,0:T(8,128)}, f32[56,8192]{1,0:T(8,128)}) custom-call(bf16[2,4,56,1024]{3,2,1,0:T(8,128)(2,1)S(1)} %copy-done.7, bf16[56,8192]{1,0:T(8,128)(2,1)S(1)} %copy-done.4, f32[56,8192]{1,0:T(8,128)S(1)} %copy-done.1, f32[56,8192]{1,0:T(8,128)S(1)} %copy-done.2), custom_call_target="tpu_custom_call" | custom-call | tf_op jit(solution)/shard_map/pallas_call | solution.py:518
  (3 shorter events, 0.0 us)
Async XLA Ops:
  0.6 1.5 %copy-start = (f32[56,8192]{1,0:T(8,128)S(1)}, f32[56,8192]{1,0:T(8,128)}, u32[]{:S(2)}) copy-start(f32[56,8192]{1,0:T(8,128)} %one_ref.3) | copy-start | bytes 5505028
  2.1 1.2 %copy-start.3 = (bf16[56,8192]{1,0:T(8,128)(2,1)S(1)}, bf16[56,8192]{1,0:T(8,128)(2,1)}, u32[]{:S(2)}) copy-start(bf16[56,8192]{1,0:T(8,128)(2,1)} %p_ref.3) | copy-start | bytes 2752516
  3.3 1.2 %copy-start.5 = (bf16[1,56,8192]{2,1,0:T(8,128)(2,1)S(1)}, bf16[1,56,8192]{2,1,0:T(8,128)(2,1)}, u32[]{:S(2)}) copy-start(bf16[1,56,8192]{2,1,0:T(8,128)(2,1)} %param.8) | copy-start | bytes 2752516
  4.5 0.7 copy-start.8
  5.2 0.7 copy-start.9
  5.9 0.7 copy-start.10
  6.5 81.7 %copy-start.1 = (f32[56,8192]{1,0:T(8,128)S(1)}, f32[56,8192]{1,0:T(8,128)}, u32[]{:S(2)}) copy-start(f32[56,8192]{1,0:T(8,128)} %one_ref.3) | copy-start | bytes 5505028
  6.5 81.7 %copy-start.4 = (bf16[56,8192]{1,0:T(8,128)(2,1)S(1)}, bf16[56,8192]{1,0:T(8,128)(2,1)}, u32[]{:S(2)}) copy-start(bf16[56,8192]{1,0:T(8,128)(2,1)} %p_ref.3) | copy-start | bytes 2752516
  86.5 0.9 copy-start.6
  88.3 1.5 %copy-start.2 = (f32[56,8192]{1,0:T(8,128)S(1)}, f32[56,8192]{1,0:T(8,128)}, u32[]{:S(2)}) copy-start(f32[56,8192]{1,0:T(8,128)} %two_ref.3) | copy-start | bytes 5505028
  89.8 1.2 %copy-start.7 = (bf16[2,4,56,1024]{3,2,1,0:T(8,128)(2,1)S(1)}, bf16[2,4,56,1024]{3,2,1,0:T(8,128)(2,1)}, u32[]{:S(2)}) copy-start(bf16[2,4,56,1024]{3,2,1,0:T(8,128)(2,1)} %copy-done.6) | copy-start | bytes 2752516

commit v4 on v3

--- a/solution.py
+++ b/solution.py
@@ -132,7 +132,6 @@
         self.edge, self.mid, self.inner = edge, mid, jnp.logical_not(edge | mid)
         self.core, self.inward, self.outward, self.other = core, inward, outward, other
         self.out_ref, self.own, self.pre, self.land, self.part = out_ref, own, pre, land, part
-        self.to_slot = jnp.where(mid, 1, 0)
 
         def span(core_of, k):
             return pl.ds(pl.multiple_of(core_of * half + k * size, size), size)
@@ -168,21 +167,30 @@
         for k in range(CHUNKS):
             self.pre_copy(k).start()
 
-    def inbound(self, k):
-        self.load(k).wait()
-        self.pre_copy(k).wait_recv()
-
+    def edge_in(self):
         @pl.when(self.edge)
         def _():
-            self.part[k] = (self.own[k].astype(f32) + self.pre[k].astype(f32)).astype(bf16)
-
-        @pl.when(jnp.logical_not(self.edge))
+            for k in range(CHUNKS):
+                self.load(k).wait()
+                self.pre_copy(k).wait_recv()
+                self.part[k] = (self.own[k].astype(f32) + self.pre[k].astype(f32)).astype(bf16)
+                self.in_copy(k, 0).start()
+
+    def pass_in(self, role, slot, k):
+        @pl.when(role)
         def _():
+            self.load(k).wait()
+            self.pre_copy(k).wait_recv()
+            total = self.own[k].astype(f32) + self.pre[k].astype(f32)
             self.in_copy(k, 0).wait_recv()
-            total = self.own[k].astype(f32) + self.pre[k].astype(f32)
             self.part[k] = (total + self.land[0, k].astype(f32)).astype(bf16)
-
-        self.in_copy(k, self.to_slot).start()
+            self.in_copy(k, slot).start()
+
+    def inner_in(self, k):
+        self.pass_in(self.inner, 0, k)
+
+    def mid_in(self, k):
+        self.pass_in(self.mid, 1, k)
 
     def middle(self, k):
         @pl.when(self.mid)
@@ -210,7 +218,7 @@
         for k in range(CHUNKS):
             self.core_copy(k, 1 - self.core).wait_recv()
             self.pre_copy(k).wait_send()
-            self.in_copy(k, self.to_slot).wait_send()
+            self.in_copy(k, 0).wait_send()
             self.core_copy(k, self.core).wait_send()
 
         @pl.when(jnp.logical_not(self.edge))
@@ -227,10 +235,11 @@
 
 
 def main_kernel(
-    tok_ref, ids_ref, gate_ref, g_ref, p_ref, one_ref, two_ref, w_ref,
+    tok_any, ids_any, gate_any, g_ref, p_ref, one_ref, two_ref, w_ref,
     sum_ref, out_ref,
-    own, landing, wide_rows, gathered, w_raw, w_tmp, w_both,
-    p_half, one_half, two_half, q_send, rows_all, hid_own, hid_all, acc, sent, came, turned, both,
+    tok_ref, ids_ref, gate_ref, own, landing, wide_rows, gathered, w_raw, w_tmp, w_both,
+    p_half, one_half, two_half, q_first, q_last, rows_first, rows_last,
+    hid_own, hid_all, acc, sent, came, turned,
     ld, sems, rs, rr, ls, lr, hsems, ys, yr, cs, cr, s1, r1, s2, r2, *rest
 ):
     x, zh, y = place()
@@ -240,17 +249,28 @@
     expert = x * ZH + zh
     rows, columns = p_ref.shape
     half = columns // 2
-    width = tok_ref.shape[1]
+    width = tok_any.shape[1]
     per = EXPERTS // 2
     batches, fit = 2, per // 2
+    q_send, rows_all = (q_first, q_last), (rows_first, rows_last)
     adding = Sum(g_ref, sum_ref, *rest)
 
     count = adding.greet()
     column = [device(x, zh, (y + k) % Y) for k in range(1, Y)]
-    near = [device(x, 1 - zh, y)] + [device((x + k) % X, zh, y) for k in range(1, X)]
-    for where in column + near:
+    plane = []
+    for k in range(1, XZ):
+        to = (expert + k) % XZ
+        plane.append(device(to // ZH, to % ZH, y))
+    for where in column + plane:
         signal(where)
 
+    small_loads = [
+        pltpu.make_async_copy(tok_any, tok_ref, ld.at[4]),
+        pltpu.make_async_copy(ids_any, ids_ref, ld.at[5]),
+        pltpu.make_async_copy(gate_any, gate_ref, ld.at[6]),
+    ]
+    for copy in small_loads:
+        copy.start()
     span = pl.ds(pl.multiple_of(core * half, half), half)
     w_load = pltpu.make_async_copy(w_ref, w_raw, ld.at[0])
     state_loads = [
@@ -264,6 +284,8 @@
     for copy in state_loads:
         copy.start()
 
+    for copy in small_loads:
+        copy.wait()
     own[:, :width] = tok_ref[...]
     lane = lax.broadcasted_iota(jnp.int32, (2, QBLOCK), 1)
     weights = jnp.zeros((2, QBLOCK), f32)
@@ -271,12 +293,13 @@
         gate = gate_ref[:, k : k + 1].astype(f32)
         weights += jnp.where(ids_ref[:, k : k + 1] == lane, gate, 0.0)
     own[:, width:] = weights.astype(bf16)
-    pl.semaphore_wait(pltpu.get_barrier_semaphore(), count + len(column) + len(near))
+    pl.semaphore_wait(pltpu.get_barrier_semaphore(), count + len(column) + len(plane))
 
     gather = Gather(own, landing, sems)
     ring = Ring(gathered, own.shape[1] // 256 * 128, rs, rr, ls, lr)
     gather.start()
     adding.start()
+    adding.edge_in()
 
     w_load.wait()
     piece = w_tmp.shape[0]
@@ -291,7 +314,7 @@
     lax.fori_loop(0, w_raw.shape[0] // piece, split, 0)
 
     gather.turn()
-    adding.inbound(0)
+    adding.inner_in(0)
     gather.finish()
     for j in range(XZ):
         for i in range(2):
@@ -302,7 +325,6 @@
         copy.wait()
 
     def quantize(k):
-        batch, spot = k // fit, k % fit
         for b in range(Y):
             cut = slice(k * Y * QBLOCK + b * QBLOCK, k * Y * QBLOCK + (b + 1) * QBLOCK)
             grad = sum_ref[core, k, :, b * QBLOCK : (b + 1) * QBLOCK].astype(f32)
@@ -310,20 +332,21 @@
             amax = jnp.max(jnp.abs(updated), axis=1, keepdims=True)
             scale = ((amax + amax_eps) / quant_limit).astype(bf16)
             quanta = (updated * (1.0 / scale.astype(f32))).astype(bf16)
-            q_send[batch, b, :, spot * QBLOCK : (spot + 1) * QBLOCK] = quanta
-            q_send[batch, b, :, fit * QBLOCK + spot : fit * QBLOCK + spot + 1] = scale
+            spot = k % fit
+            q_send[k // fit][b, :, spot * QBLOCK : (spot + 1) * QBLOCK] = quanta
+            q_send[1][b, :, fit * QBLOCK + k : fit * QBLOCK + k + 1] = scale
 
     order = [1, 7, 2, 6, 3, 5, 4]
 
     def relay(batch, k):
         return remote(
-            q_send.at[batch, (y + k) % Y], rows_all.at[core, batch, y],
+            q_send[batch].at[(y + k) % Y], rows_all[batch].at[core, y],
             ys.at[batch, k], yr.at[batch, k], column[k - 1],
         )
 
     def mine(batch):
         return pltpu.make_async_copy(
-            q_send.at[batch, y], rows_all.at[core, batch, y], ys.at[batch, 0]
+            q_send[batch].at[y], rows_all[batch].at[core, y], ys.at[batch, 0]
         )
 
     def relay_start(batch):
@@ -332,7 +355,7 @@
         mine(batch).start()
 
     def share(batch, which):
-        part = rows_all.at[which, batch]
+        part = rows_all[batch].at[which]
         return remote(part, part, cs.at[batch], cr.at[batch], other)
 
     def relay_finish(batch):
@@ -341,29 +364,32 @@
             relay(batch, k).wait_recv()
         share(batch, core).start()
 
-    adding.inbound(1)
-    adding.inbound(2)
-    adding.middle(0)
+    adding.inner_in(1)
+    adding.inner_in(2)
+    adding.mid_in(0)
+    adding.mid_in(1)
     ring.wait(0)
     ring.start(1)
-    adding.inbound(3)
+    adding.inner_in(3)
+    adding.mid_in(2)
+    adding.middle(0)
     adding.middle(1)
-    adding.middle(2)
-    adding.inner_out(0)
+    adding.mid_in(3)
     ring.wait(1)
     ring.start(2)
+    adding.middle(2)
     adding.middle(3)
+    adding.inner_out(0)
     adding.inner_out(1)
-    adding.inner_out(2)
-    adding.edge_out(0)
     ring.wait(2)
     ring.start(3)
+    adding.inner_out(2)
+    adding.inner_out(3)
+    adding.edge_out(0)
     quantize(0)
-    adding.inner_out(3)
     adding.edge_out(1)
     quantize(1)
     relay_start(0)
-    adding.edge_out(2)
     ring.wait(3)
 
     tokens = gathered.reshape(Y * 16, own.shape[1])
@@ -376,8 +402,9 @@
     hid_own[...] = jnp.transpose(hidden).astype(bf16)
     hid_gather = Gather(hid_own, hid_all, hsems)
     hid_gather.start()
+    adding.edge_out(2)
+    quantize(2)
     adding.edge_out(3)
-    quantize(2)
     quantize(3)
     relay_start(1)
     relay_finish(0)
@@ -385,27 +412,23 @@
     relay_finish(1)
     hid_gather.finish()
 
-    def products(which, batch):
-        for j in range(Y):
-            total = None
-            for e in range(fit):
-                quanta = rows_all[which, batch, j, :, e * QBLOCK : (e + 1) * QBLOCK]
-                scale = rows_all[which, batch, j, :, fit * QBLOCK + e : fit * QBLOCK + e + 1]
-                term = scale.astype(f32) * jnp.dot(
-                    quanta, hid_all[which * per + batch * fit + e], preferred_element_type=f32
-                )
-                total = term if total is None else total + term
-            yield j, total
-
-    for j, total in products(core, 0):
-        acc[j, :rows] = total
+    def products(which, j):
+        total = None
+        for e in range(per):
+            spot = e % fit
+            quanta = rows_all[e // fit][which, j, :, spot * QBLOCK : (spot + 1) * QBLOCK]
+            scale = rows_all[1][which, j, :, fit * QBLOCK + e : fit * QBLOCK + e + 1].astype(f32)
+            term = scale * jnp.dot(quanta, hid_all[which * per + e], preferred_element_type=f32)
+            total = term if total is None else total + term
+        return total
+
+    for j in range(Y):
+        acc[j, :rows] = products(core, j)
         acc[j, rows:] = jnp.zeros_like(acc[j, rows:])
-    for j, total in products(core, 1):
-        acc[j, :rows] += total
     for batch in range(batches):
         share(batch, 1 - core).wait_recv()
-        for j, total in products(1 - core, batch):
-            acc[j, :rows] += total
+    for j in range(Y):
+        acc[j, :rows] += products(1 - core, j)
 
     for j in range(Y // 2):
         pair = jnp.concatenate([acc[2 * j], acc[2 * j + 1]], axis=0)
@@ -426,19 +449,13 @@
     for i in range(2):
         for q in range(4):
             part = total[i * 8 : (i + 1) * 8, q * 128 : (q + 1) * 128]
-            for j in range(XZ):
-                turned[j % ZH, j // ZH, i * 4 + q : i * 4 + q + 1, :] = part[j : j + 1]
-    cross = remote(turned.at[1 - zh], both.at[zh], s2.at[0], r2.at[0], near[0])
-    cross.start()
-    both[pl.ds(zh, 1)] = turned[pl.ds(zh, 1)]
-    cross.wait()
+            turned[:, i * 4 + q, :] = part
     copies = []
-    for k in range(1, X):
-        src = both.at[:, (x + k) % X]
-        copies.append(remote(src, out_ref.at[:, x], s2.at[k], r2.at[k], near[k]))
+    for k in range(1, XZ):
+        to = (expert + k) % XZ
+        copies.append(remote(turned.at[to], out_ref.at[expert], s2.at[k], r2.at[k], plane[k - 1]))
         copies[-1].start()
-    for i in range(ZH):
-        out_ref[i, pl.ds(x, 1)] = both[i, pl.ds(x, 1)]
+    out_ref[pl.ds(expert, 1)] = turned[pl.ds(expert, 1)]
     for copy in copies:
         copy.wait()
 
@@ -474,11 +491,14 @@
         main_kernel,
         out_shape=(
             shape((2, CHUNKS, rows, size), bf16),
-            shape((ZH, X, 8, 128), f32),
+            shape((XZ, 8, 128), f32),
         ),
-        in_specs=[VMEM] * 3 + [ANY] * 5,
+        in_specs=[ANY] * 8,
         out_specs=(VMEM, VMEM),
         scratch_shapes=[
+            pltpu.VMEM(tokens.shape, bf16),
+            pltpu.VMEM(expert_ids.shape, jnp.int32),
+            pltpu.VMEM(gate_vals.shape, bf16),
             pltpu.VMEM((2, full), bf16),
             pltpu.VMEM((XZ, 2, full), bf16),
             pltpu.VMEM((16, full), f32),
@@ -489,25 +509,26 @@
             pltpu.VMEM((rows, half), bf16),
             pltpu.VMEM((rows, half), f32),
             pltpu.VMEM((rows, half), f32),
+            pltpu.VMEM((Y, rows, 2 * QBLOCK), bf16),
+            pltpu.VMEM((Y, rows, 3 * QBLOCK), bf16),
+            pltpu.VMEM((2, Y, rows, 2 * QBLOCK), bf16),
             pltpu.VMEM((2, Y, rows, 3 * QBLOCK), bf16),
-            pltpu.VMEM((2, 2, Y, rows, 3 * QBLOCK), bf16),
             pltpu.VMEM((QBLOCK, tok), bf16),
             pltpu.VMEM((XZ, QBLOCK, tok), bf16),
             pltpu.VMEM((Y, 64, tok), f32),
             pltpu.VMEM((Y, 16, 512), bf16),
             pltpu.VMEM((Y, 16, 512), bf16),
-            pltpu.VMEM((ZH, X, 8, 128), f32),
-            pltpu.VMEM((ZH, X, 8, 128), f32),
-            DMA((4,)),
+            pltpu.VMEM((XZ, 8, 128), f32),
+            DMA((7,)),
         ]
         + GATHER_SEMS
         + RING_SEMS
         + GATHER_SEMS
-        + [DMA((2, 8)), DMA((2, 8)), DMA((2,)), DMA((2,)), DMA((8,)), DMA((8,)), DMA((4,)), DMA((4,))]
+        + [DMA((2, 8)), DMA((2, 8)), DMA((2,)), DMA((2,)), DMA((8,)), DMA((8,)), DMA((8,)), DMA((8,))]
         + [chunk, chunk, pltpu.VMEM((2, CHUNKS, rows, size), bf16), chunk]
         + [sem, sem, sem, sem, DMA((2, CHUNKS)), sem, sem, sem, sem],
         compiler_params=pltpu.CompilerParams(
-            collective_id=0, has_side_effects=True, vmem_limit_bytes=48 * 2**20
+            collective_id=0, has_side_effects=True, vmem_limit_bytes=62 * 2**20
         ),
     )(
         tokens, expert_ids, gate_vals, grad_parts[0], master, moment_one, moment_two,
@@ -525,10 +546,10 @@
         ),
         in_specs=[pl.BlockSpec((1, 1, rows, size), lambda e: (e // CHUNKS, e % CHUNKS, 0, 0)), spec, spec, spec],
         out_specs=(spec, spec, spec),
-        compiler_params=pltpu.CompilerParams(vmem_limit_bytes=40 * 2**20),
+        compiler_params=pltpu.CompilerParams(vmem_limit_bytes=62 * 2**20),
     )(total, master, moment_one, moment_two)
 
-    done = done.reshape(ZH, X, 2, Y, 64)[..., :rows].transpose(2, 1, 0, 3, 4).reshape(2, width)
+    done = done.reshape(XZ, 2, Y, 64)[..., :rows].transpose(1, 0, 2, 3).reshape(2, width)
     return new_master, new_one, new_two, done.astype(bf16)
 
 

time: 95.5 us -> 86.6 us (0.907)
  the two profiles are of different devices: /device:TPU:128 before, /device:TPU:1 now
where the time goes in v4:
time: 86.6 us; the launch traced here: 86.3 us
  Pallas kernels  84.1 us (97%)
    pallas_call x1, Pallas kernels, body(): pl.pallas_call(main_kernel, out_shape=(shape((2, CHUNKS, rows, size), bf1...  76.6 us
    pallas_call x1, Pallas kernels, body(): pl.pallas_call(adam_kernel, grid=(2 * CHUNKS,), out_shape=(shape((rows, c...  7.46 us

profile of v4, /device:TPU:1, one launch (start us, length us, event | category | flops | bytes accessed | tf_op | source)
XLA Modules:
  0.0 86.3 jit_solution(14565691415107067747)
XLA Ops:
  0.6 76.6 %shard_map.111 = (bf16[2,4,56,1024]{3,2,1,0:T(8,128)(2,1)}, f32[8,8,128]{2,1,0:T(8,128)}) custom-call(bf16[2,3584]{1,0:T(2,128)(2,1)} %tok_any.1, s32[2,4]{1,0:T(2,128)} %ids_any.1, bf16[2,4]{1,0:T(2,128)(2,1)} %gate_any.1, bf16[56,8192]{1,0:T(8,128)(2,1)} %bitcast.7, bf16[56,8192]{1,0:T(8,128)(2,1)} %p_ref.3, f32[56,8192]{1,0:T(8,128)} %one_ref.3, ...), custom_call_target="tpu_custom_call" | custom-call | tf_op jit(solution)/shard_map/pallas_call | solution.py:490
  77.2 0.8 convert.4
  78.0 0.1 reshape.18
  78.1 0.7 convert_element_type.8
  78.8 7.5 %shard_map.112 = (bf16[56,8192]{1,0:T(8,128)(2,1)}, f32[56,8192]{1,0:T(8,128)}, f32[56,8192]{1,0:T(8,128)}) custom-call(bf16[2,4,56,1024]{3,2,1,0:T(8,128)(2,1)} %get-tuple-element.9.g_ref, bf16[56,8192]{1,0:T(8,128)(2,1)} %p_ref.3, f32[56,8192]{1,0:T(8,128)} %one_ref.3, f32[56,8192]{1,0:T(8,128)} %two_ref.3), custom_call_target="tpu_custom_call" | custom-call | tf_op jit(solution)/shard_map/pallas_call | solution.py:539
  (2 shorter events, 0.0 us)

commit v5 on v4

--- a/solution.py
+++ b/solution.py
@@ -22,7 +22,7 @@
 bias_second = 1.0 - 0.95**10
 
 VMEM = pl.BlockSpec(memory_space=pltpu.VMEM)
-ANY = pl.BlockSpec(memory_space=pl.ANY)
+HBM = pl.BlockSpec(memory_space=pltpu.HBM)
 DMA = pltpu.SemaphoreType.DMA
 f32 = jnp.float32
 bf16 = jnp.bfloat16
@@ -216,7 +216,6 @@
 
     def finish(self):
         for k in range(CHUNKS):
-            self.core_copy(k, 1 - self.core).wait_recv()
             self.pre_copy(k).wait_send()
             self.in_copy(k, 0).wait_send()
             self.core_copy(k, self.core).wait_send()
@@ -236,9 +235,9 @@
 
 def main_kernel(
     tok_any, ids_any, gate_any, g_ref, p_ref, one_ref, two_ref, w_ref,
-    sum_ref, out_ref,
+    newp_ref, newone_ref, newtwo_ref, out_ref,
     tok_ref, ids_ref, gate_ref, own, landing, wide_rows, gathered, w_raw, w_tmp, w_both,
-    p_half, one_half, two_half, q_first, q_last, rows_first, rows_last,
+    sum_ref, final, q_first, q_last, rows_first, rows_last,
     hid_own, hid_all, acc, sent, came, turned,
     ld, sems, rs, rr, ls, lr, hsems, ys, yr, cs, cr, s1, r1, s2, r2, *rest
 ):
@@ -265,19 +264,22 @@
         signal(where)
 
     small_loads = [
-        pltpu.make_async_copy(tok_any, tok_ref, ld.at[4]),
-        pltpu.make_async_copy(ids_any, ids_ref, ld.at[5]),
-        pltpu.make_async_copy(gate_any, gate_ref, ld.at[6]),
+        pltpu.make_async_copy(tok_any, tok_ref, ld.at[7]),
+        pltpu.make_async_copy(ids_any, ids_ref, ld.at[8]),
+        pltpu.make_async_copy(gate_any, gate_ref, ld.at[9]),
     ]
     for copy in small_loads:
         copy.start()
-    span = pl.ds(pl.multiple_of(core * half, half), half)
     w_load = pltpu.make_async_copy(w_ref, w_raw, ld.at[0])
-    state_loads = [
-        pltpu.make_async_copy(p_ref.at[:, span], p_half, ld.at[1]),
-        pltpu.make_async_copy(one_ref.at[:, span], one_half, ld.at[2]),
-        pltpu.make_async_copy(two_ref.at[:, span], two_half, ld.at[3]),
-    ]
+    state_loads = []
+    for i, which in enumerate((core, 1 - core)):
+        span = pl.ds(pl.multiple_of(which * half, half), half)
+        for n, (src, dst) in enumerate(
+            ((p_ref, newp_ref), (one_ref, newone_ref), (two_ref, newtwo_ref))
+        ):
+            state_loads.append(
+                pltpu.make_async_copy(src.at[:, span], dst.at[:, span], ld.at[1 + i * 3 + n])
+            )
     for k in range(CHUNKS):
         adding.load(k).start()
     w_load.start()
@@ -324,11 +326,23 @@
     for copy in state_loads:
         copy.wait()
 
+    def advance(which, k, b):
+        at = which * half + (k * Y + b) * QBLOCK
+        cut = pl.ds(pl.multiple_of(at, QBLOCK), QBLOCK)
+        one, two, updated = adam(
+            sum_ref[which, k, :, b * QBLOCK : (b + 1) * QBLOCK].astype(f32),
+            newp_ref[:, cut].astype(f32),
+            newone_ref[:, cut],
+            newtwo_ref[:, cut],
+        )
+        newone_ref[:, cut] = one
+        newtwo_ref[:, cut] = two
+        newp_ref[:, cut] = updated.astype(bf16)
+        return updated
+
     def quantize(k):
         for b in range(Y):
-            cut = slice(k * Y * QBLOCK + b * QBLOCK, k * Y * QBLOCK + (b + 1) * QBLOCK)
-            grad = sum_ref[core, k, :, b * QBLOCK : (b + 1) * QBLOCK].astype(f32)
-            _, _, updated = adam(grad, p_half[:, cut].astype(f32), one_half[:, cut], two_half[:, cut])
+            updated = advance(core, k, b)
             amax = jnp.max(jnp.abs(updated), axis=1, keepdims=True)
             scale = ((amax + amax_eps) / quant_limit).astype(bf16)
             quanta = (updated * (1.0 / scale.astype(f32))).astype(bf16)
@@ -441,6 +455,14 @@
         copies.append(remote(sent.at[to], came.at[y], s1.at[k], r1.at[k], column[k - 1]))
         copies[-1].start()
     came[pl.ds(y, 1)] = sent[pl.ds(y, 1)]
+
+    def other_half(k):
+        adding.core_copy(k, 1 - core).wait_recv()
+        for b in range(Y):
+            advance(1 - core, k, b)
+
+    other_half(0)
+    other_half(1)
     for copy in copies:
         copy.wait()
     total = came[0].astype(f32)
@@ -453,11 +475,14 @@
     copies = []
     for k in range(1, XZ):
         to = (expert + k) % XZ
-        copies.append(remote(turned.at[to], out_ref.at[expert], s2.at[k], r2.at[k], plane[k - 1]))
+        copies.append(remote(turned.at[to], final.at[expert], s2.at[k], r2.at[k], plane[k - 1]))
         copies[-1].start()
-    out_ref[pl.ds(expert, 1)] = turned[pl.ds(expert, 1)]
+    final[pl.ds(expert, 1)] = turned[pl.ds(expert, 1)]
+    other_half(2)
+    other_half(3)
     for copy in copies:
         copy.wait()
+    out_ref[...] = final[...].astype(bf16)
 
     for batch in range(batches):
         for k in order:
@@ -466,35 +491,25 @@
     adding.finish()
 
 
-def adam_kernel(g_ref, p_ref, one_ref, two_ref, newp_ref, newone_ref, newtwo_ref):
-    for b in range(g_ref.shape[3] // QBLOCK):
-        cut = slice(b * QBLOCK, (b + 1) * QBLOCK)
-        one, two, updated = adam(
-            g_ref[0, 0, :, cut].astype(f32), p_ref[:, cut].astype(f32), one_ref[:, cut], two_ref[:, cut]
-        )
-        newone_ref[:, cut] = one
-        newtwo_ref[:, cut] = two
-        newp_ref[:, cut] = updated.astype(bf16)
-
-
 def body(grad_parts, master, moment_one, moment_two, gate_up, tokens, expert_ids, gate_vals):
     shape = jax.ShapeDtypeStruct
     rows, columns = master.shape
     width = tokens.shape[1]
     full = width + QBLOCK
-    half = columns // 2
-    size = half // CHUNKS
+    size = columns // 2 // CHUNKS
     tok = Y * 16
     sem = DMA((CHUNKS,))
     chunk = pltpu.VMEM((CHUNKS, rows, size), bf16)
-    total, done = pl.pallas_call(
+    new_master, new_one, new_two, done = pl.pallas_call(
         main_kernel,
         out_shape=(
-            shape((2, CHUNKS, rows, size), bf16),
-            shape((XZ, 8, 128), f32),
+            shape((rows, columns), bf16),
+            shape((rows, columns), f32),
+            shape((rows, columns), f32),
+            shape((XZ, 8, 128), bf16),
         ),
-        in_specs=[ANY] * 8,
-        out_specs=(VMEM, VMEM),
+        in_specs=[HBM] * 8,
+        out_specs=(VMEM,) * 4,
         scratch_shapes=[
             pltpu.VMEM(tokens.shape, bf16),
             pltpu.VMEM(expert_ids.shape, jnp.int32),
@@ -506,9 +521,8 @@
             pltpu.VMEM((2 * width, QBLOCK), bf16),
             pltpu.VMEM((512, QBLOCK), f32),
             pltpu.VMEM((width, 2 * QBLOCK), bf16),
-            pltpu.VMEM((rows, half), bf16),
-            pltpu.VMEM((rows, half), f32),
-            pltpu.VMEM((rows, half), f32),
+            pltpu.VMEM((2, CHUNKS, rows, size), bf16),
+            pltpu.VMEM((XZ, 8, 128), f32),
             pltpu.VMEM((Y, rows, 2 * QBLOCK), bf16),
             pltpu.VMEM((Y, rows, 3 * QBLOCK), bf16),
             pltpu.VMEM((2, Y, rows, 2 * QBLOCK), bf16),
@@ -519,7 +533,7 @@
             pltpu.VMEM((Y, 16, 512), bf16),
             pltpu.VMEM((Y, 16, 512), bf16),
             pltpu.VMEM((XZ, 8, 128), f32),
-            DMA((7,)),
+            DMA((10,)),
         ]
         + GATHER_SEMS
         + RING_SEMS
@@ -528,29 +542,20 @@
         + [chunk, chunk, pltpu.VMEM((2, CHUNKS, rows, size), bf16), chunk]
         + [sem, sem, sem, sem, DMA((2, CHUNKS)), sem, sem, sem, sem],
         compiler_params=pltpu.CompilerParams(
-            collective_id=0, has_side_effects=True, vmem_limit_bytes=62 * 2**20
+            collective_id=0, has_side_effects=True, vmem_limit_bytes=36 * 2**20
         ),
     )(
-        tokens, expert_ids, gate_vals, grad_parts[0], master, moment_one, moment_two,
-        gate_up.reshape(2 * width, QBLOCK),
+        *[
+            pltpu.with_memory_space_constraint(value, pltpu.HBM)
+            for value in (
+                tokens, expert_ids, gate_vals, grad_parts[0], master, moment_one, moment_two,
+                gate_up.reshape(2 * width, QBLOCK),
+            )
+        ]
     )
 
-    spec = pl.BlockSpec((rows, size), lambda e: (0, e))
-    new_master, new_one, new_two = pl.pallas_call(
-        adam_kernel,
-        grid=(2 * CHUNKS,),
-        out_shape=(
-            shape((rows, columns), bf16),
-            shape((rows, columns), f32),
-            shape((rows, columns), f32),
-        ),
-        in_specs=[pl.BlockSpec((1, 1, rows, size), lambda e: (e // CHUNKS, e % CHUNKS, 0, 0)), spec, spec, spec],
-        out_specs=(spec, spec, spec),
-        compiler_params=pltpu.CompilerParams(vmem_limit_bytes=62 * 2**20),
-    )(total, master, moment_one, moment_two)
-
     done = done.reshape(XZ, 2, Y, 64)[..., :rows].transpose(1, 0, 2, 3).reshape(2, width)
-    return new_master, new_one, new_two, done.astype(bf16)
+    return new_master, new_one, new_two, done
 
 
 def solution(mesh):

time: 86.6 us -> 82.8 us (0.956)
  Pallas kernels: 84.1 us -> 75.6 us
  local copies, waits for them, and re-layouts: 0.81 us -> 6.31 us
    pallas_call x2 -> x1, Pallas kernels: 84.1 us -> 75.6 us  [body(): pl.pallas_call(main_kernel, out_shape=(shape((rows, columns), bf16), shap...]
    unnamed x0 -> x7, local copies, waits for them, and re-layouts: none -> 5.51 us
where the time goes in v5:
time: 82.8 us; the launch traced here: 82.6 us
  Pallas kernels  75.6 us (91%)
  local copies, waits for them, and re-layouts  6.31 us (8%)
    pallas_call x1, Pallas kernels, body(): pl.pallas_call(main_kernel, out_shape=(shape((rows, columns), bf16), shap...  75.6 us
    unnamed x7, local copies, waits for them, and re-layouts  5.51 us

profile of v5, /device:TPU:1, one launch (start us, length us, event | category | flops | bytes accessed | tf_op | source)
XLA Modules:
  0.0 82.6 jit_solution(7970051525491459987)
XLA Ops:
  0.6 75.6 %shard_map.111 = (bf16[56,8192]{1,0:T(8,128)(2,1)S(1)}, f32[56,8192]{1,0:T(8,128)S(1)}, f32[56,8192]{1,0:T(8,128)S(1)}, bf16[8,8,128]{2,1,0:T(8,128)(2,1)S(1)}) custom-call(bf16[2,3584]{1,0:T(2,128)(2,1)} %tok_any.1, s32[2,4]{1,0:T(2,128)} %ids_any.1, bf16[2,4]{1,0:T(2,128)(2,1)} %gate_any.1, bf16[56,8192]{1,0:T(8,128)(2,1)} %bitcast.7, ...), custom_call_target="tpu_custom_call" | custom-call | tf_op jit(solution)/shard_map/pallas_call | solution.py:503
  76.3 0.0 copy-start
  76.3 1.2 %copy-done = f32[56,8192]{1,0:T(8,128)} copy-done((f32[56,8192]{1,0:T(8,128)}, f32[56,8192]{1,0:T(8,128)S(1)}, u32[]{:S(2)}) %copy-start) | copy-done | bytes 1835032
  77.5 0.1 reshape.18
  77.6 0.7 reshape.19
  78.3 0.0 copy-start.1
  78.3 0.9 %copy.16 = bf16[56,8192]{1,0:T(8,128)(2,1)} copy(bf16[56,8192]{1,0:T(8,128)(2,1)S(1)} %get-tuple-element.16) | data formatting | bytes 1835008
  79.3 0.9 %copy-done.1 = f32[56,8192]{1,0:T(8,128)S(1)} copy-done((f32[56,8192]{1,0:T(8,128)S(1)}, f32[56,8192]{1,0:T(8,128)}, u32[]{:S(2)}) %copy-start.1) | copy-done | bytes 1835032
  80.2 1.2 %copy.17 = f32[56,8192]{1,0:T(8,128)} copy(f32[56,8192]{1,0:T(8,128)S(1)} %copy-done.1) | data formatting | bytes 3670016
  81.4 1.2 %copy.18 = f32[56,8192]{1,0:T(8,128)} copy(f32[56,8192]{1,0:T(8,128)S(1)} %get-tuple-element.18) | data formatting | bytes 3670016
  (2 shorter events, 0.0 us)
Async XLA Ops:
  76.3 1.2 %copy-start = (f32[56,8192]{1,0:T(8,128)}, f32[56,8192]{1,0:T(8,128)S(1)}, u32[]{:S(2)}) copy-start(f32[56,8192]{1,0:T(8,128)S(1)} %get-tuple-element.17) | copy-start | bytes 5505028
  78.3 1.8 %copy-start.1 = (f32[56,8192]{1,0:T(8,128)S(1)}, f32[56,8192]{1,0:T(8,128)}, u32[]{:S(2)}) copy-start(f32[56,8192]{1,0:T(8,128)} %copy-done) | copy-start | bytes 5505028

commit v6 on v5

--- a/solution.py
+++ b/solution.py
@@ -482,13 +482,45 @@
     other_half(3)
     for copy in copies:
         copy.wait()
-    out_ref[...] = final[...].astype(bf16)
+    assemble(final, out_ref, rows)
 
     for batch in range(batches):
         for k in order:
             relay(batch, k).wait_send()
         share(batch, core).wait_send()
     adding.finish()
+
+
+def assemble(final, out_ref, rows):
+    lane = lax.broadcasted_iota(jnp.int32, (2, 128), 1)
+    pieces = [None] * (out_ref.shape[1] // 128)
+
+    def add(tile, value):
+        pieces[tile] = value if pieces[tile] is None else pieces[tile] + value
+
+    for j in range(XZ):
+        for q in range(4):
+            pair = final[j, pl.ds(q, 2, stride=4), :]
+            closed = jnp.where(lane < rows, pair, pltpu.roll(pair, 64 + rows, 1))
+            closed = jnp.where(lane < 2 * rows, closed, 0.0)
+            tile, shift = divmod((j * 4 + q) * 2 * rows, 128)
+            turned = pltpu.roll(closed, shift, 1) if shift else closed
+            add(tile, jnp.where(lane >= shift, turned, 0.0))
+            if shift + 2 * rows > 128:
+                add(tile + 1, jnp.where(lane < shift, turned, 0.0))
+    for tile, value in enumerate(pieces):
+        out_ref[:, tile * 128 : (tile + 1) * 128] = value.astype(bf16)
+
+
+def store_kernel(*refs):
+    sources, targets, sems = refs[:4], refs[4:8], refs[8]
+    copies = [
+        pltpu.make_async_copy(src, dst, sems.at[i]) for i, (src, dst) in enumerate(zip(sources, targets))
+    ]
+    for copy in copies:
+        copy.start()
+    for copy in copies:
+        copy.wait()
 
 
 def body(grad_parts, master, moment_one, moment_two, gate_up, tokens, expert_ids, gate_vals):
@@ -500,13 +532,13 @@
     tok = Y * 16
     sem = DMA((CHUNKS,))
     chunk = pltpu.VMEM((CHUNKS, rows, size), bf16)
-    new_master, new_one, new_two, done = pl.pallas_call(
+    results = pl.pallas_call(
         main_kernel,
         out_shape=(
             shape((rows, columns), bf16),
             shape((rows, columns), f32),
             shape((rows, columns), f32),
-            shape((XZ, 8, 128), bf16),
+            shape((2, width), bf16),
         ),
         in_specs=[HBM] * 8,
         out_specs=(VMEM,) * 4,
@@ -554,8 +586,15 @@
         ]
     )
 
-    done = done.reshape(XZ, 2, Y, 64)[..., :rows].transpose(1, 0, 2, 3).reshape(2, width)
-    return new_master, new_one, new_two, done
+    anywhere = pl.BlockSpec(memory_space=pl.ANY)
+    return pl.pallas_call(
+        store_kernel,
+        out_shape=tuple(shape(value.shape, value.dtype) for value in results),
+        in_specs=[VMEM] * 4,
+        out_specs=(anywhere,) * 4,
+        scratch_shapes=[DMA((4,))],
+        compiler_params=pltpu.CompilerParams(vmem_limit_bytes=16 * 2**20),
+    )(*results)
 
 
 def solution(mesh):

time: 82.8 us -> 78.8 us (0.952)
  local copies, waits for them, and re-layouts: 6.31 us -> 0 us
  Pallas kernels: 75.6 us -> 78 us
    unnamed x7 -> x0, local copies, waits for them, and re-layouts: 5.51 us -> none
    pallas_call x0 -> x1, Pallas kernels: none -> 2.17 us  [body(): pl.pallas_call(store_kernel, out_shape=tuple((shape(value.shape, value.dt...]
where the time goes in v6:
time: 78.8 us; the launch traced here: 78.6 us
  Pallas kernels  78 us (99%)
    pallas_call x1, Pallas kernels, body(): pl.pallas_call(main_kernel, out_shape=(shape((rows, columns), bf16), shap...  75.8 us
    pallas_call x1, Pallas kernels, body(): pl.pallas_call(store_kernel, out_shape=tuple((shape(value.shape, value.dt...  2.17 us

profile of v6, /device:TPU:1, one launch (start us, length us, event | category | flops | bytes accessed | tf_op | source)
XLA Modules:
  0.0 78.6 jit_solution(2498332720100024459)
XLA Ops:
  0.6 75.8 %shard_map.111 = (bf16[56,8192]{1,0:T(8,128)(2,1)S(1)}, f32[56,8192]{1,0:T(8,128)S(1)}, f32[56,8192]{1,0:T(8,128)S(1)}, bf16[2,3584]{1,0:T(2,128)(2,1)S(1)}) custom-call(bf16[2,3584]{1,0:T(2,128)(2,1)} %tok_any.1, s32[2,4]{1,0:T(2,128)} %ids_any.1, bf16[2,4]{1,0:T(2,128)(2,1)} %gate_any.1, bf16[56,8192]{1,0:T(8,128)(2,1)} %bitcast.3, ...), custom_call_target="tpu_custom_call" | custom-call | tf_op jit(solution)/shard_map/pallas_call | solution.py:535
  76.4 2.2 %shard_map.112 = (bf16[56,8192]{1,0:T(8,128)(2,1)}, f32[56,8192]{1,0:T(8,128)}, f32[56,8192]{1,0:T(8,128)}, bf16[2,3584]{1,0:T(2,128)(2,1)}) custom-call(bf16[56,8192]{1,0:T(8,128)(2,1)S(1)} %get-tuple-element.8.refs_0_, f32[56,8192]{1,0:T(8,128)S(1)} %get-tuple-element.9.refs_1_, f32[56,8192]{1,0:T(8,128)S(1)} %get-tuple-element.10.refs_2_, ...), custom_call_target="tpu_custom_call" | custom-call | tf_op jit(solution)/shard_map/pallas_call | solution.py:590

commit v7 on v6

--- a/solution.py
+++ b/solution.py
@@ -74,7 +74,7 @@
         pair = landing.at[pl.ds(x * ZH, ZH)]
         self.along = [
             remote(pair, pair, sems.at[1 + k], sems.at[4 + k], device((x + k) % X, zh, y))
-            for k in range(1, X)
+            for k in (2, 1, 3)
         ]
 
     def start(self):
@@ -350,7 +350,7 @@
             q_send[k // fit][b, :, spot * QBLOCK : (spot + 1) * QBLOCK] = quanta
             q_send[1][b, :, fit * QBLOCK + k : fit * QBLOCK + k + 1] = scale
 
-    order = [1, 7, 2, 6, 3, 5, 4]
+    order = [4, 3, 5, 2, 6, 1, 7]
 
     def relay(batch, k):
         return remote(
@@ -473,7 +473,7 @@
             part = total[i * 8 : (i + 1) * 8, q * 128 : (q + 1) * 128]
             turned[:, i * 4 + q, :] = part
     copies = []
-    for k in range(1, XZ):
+    for k in (3, 5, 1, 7, 4, 2, 6):
         to = (expert + k) % XZ
         copies.append(remote(turned.at[to], final.at[expert], s2.at[k], r2.at[k], plane[k - 1]))
         copies[-1].start()

time: 78.8 us -> 76.5 us (0.971)
  Pallas kernels: 78 us -> 75.6 us
    pallas_call x1, Pallas kernels: 75.8 us -> 73.5 us  [body(): pl.pallas_call(main_kernel, out_shape=(shape((rows, columns), bf16), shap...]
where the time goes in v7:
time: 76.5 us; the launch traced here: 76.3 us
  Pallas kernels  75.6 us (99%)
    pallas_call x1, Pallas kernels, body(): pl.pallas_call(main_kernel, out_shape=(shape((rows, columns), bf16), shap...  73.5 us
    pallas_call x1, Pallas kernels, body(): pl.pallas_call(store_kernel, out_shape=tuple((shape(value.shape, value.dt...  2.17 us

profile of v7, /device:TPU:1, one launch (start us, length us, event | category | flops | bytes accessed | tf_op | source)
XLA Modules:
  0.0 76.3 jit_solution(6683795445623417784)
XLA Ops:
  0.6 73.5 %shard_map.111 = (bf16[56,8192]{1,0:T(8,128)(2,1)S(1)}, f32[56,8192]{1,0:T(8,128)S(1)}, f32[56,8192]{1,0:T(8,128)S(1)}, bf16[2,3584]{1,0:T(2,128)(2,1)S(1)}) custom-call(bf16[2,3584]{1,0:T(2,128)(2,1)} %tok_any.1, s32[2,4]{1,0:T(2,128)} %ids_any.1, bf16[2,4]{1,0:T(2,128)(2,1)} %gate_any.1, bf16[56,8192]{1,0:T(8,128)(2,1)} %bitcast.3, ...), custom_call_target="tpu_custom_call" | custom-call | tf_op jit(solution)/shard_map/pallas_call | solution.py:535
  74.1 2.2 %shard_map.112 = (bf16[56,8192]{1,0:T(8,128)(2,1)}, f32[56,8192]{1,0:T(8,128)}, f32[56,8192]{1,0:T(8,128)}, bf16[2,3584]{1,0:T(2,128)(2,1)}) custom-call(bf16[56,8192]{1,0:T(8,128)(2,1)S(1)} %get-tuple-element.8.refs_0_, f32[56,8192]{1,0:T(8,128)S(1)} %get-tuple-element.9.refs_1_, f32[56,8192]{1,0:T(8,128)S(1)} %get-tuple-element.10.refs_2_, ...), custom_call_target="tpu_custom_call" | custom-call | tf_op jit(solution)/shard_map/pallas_call | solution.py:590

commit v8 on v7

--- a/solution.py
+++ b/solution.py
@@ -254,14 +254,16 @@
     q_send, rows_all = (q_first, q_last), (rows_first, rows_last)
     adding = Sum(g_ref, sum_ref, *rest)
 
-    count = adding.greet()
     column = [device(x, zh, (y + k) % Y) for k in range(1, Y)]
     plane = []
     for k in range(1, XZ):
         to = (expert + k) % XZ
         plane.append(device(to // ZH, to % ZH, y))
-    for where in column + plane:
-        signal(where)
+    for k in (3, 5, 1, 7, 4, 2, 6):
+        signal(plane[k - 1])
+    for k in (4, 3, 5, 2, 6, 1, 7):
+        signal(column[k - 1])
+    count = adding.greet()
 
     small_loads = [
         pltpu.make_async_copy(tok_any, tok_ref, ld.at[7]),

time: 76.5 us -> 76.6 us (level)
  no operation moved by 1% of the time
where the time goes in v8:
time: 76.6 us; the launch traced here: 76.4 us
  Pallas kernels  75.8 us (99%)
    pallas_call x1, Pallas kernels, body(): pl.pallas_call(main_kernel, out_shape=(shape((rows, columns), bf16), shap...  73.6 us
    pallas_call x1, Pallas kernels, body(): pl.pallas_call(store_kernel, out_shape=tuple((shape(value.shape, value.dt...  2.17 us

profile of v8, /device:TPU:1, one launch (start us, length us, event | category | flops | bytes accessed | tf_op | source)
XLA Modules:
  0.0 76.4 jit_solution(7489671160065969288)
XLA Ops:
  0.6 73.6 %shard_map.111 = (bf16[56,8192]{1,0:T(8,128)(2,1)S(1)}, f32[56,8192]{1,0:T(8,128)S(1)}, f32[56,8192]{1,0:T(8,128)S(1)}, bf16[2,3584]{1,0:T(2,128)(2,1)S(1)}) custom-call(bf16[2,3584]{1,0:T(2,128)(2,1)} %tok_any.1, s32[2,4]{1,0:T(2,128)} %ids_any.1, bf16[2,4]{1,0:T(2,128)(2,1)} %gate_any.1, bf16[56,8192]{1,0:T(8,128)(2,1)} %bitcast.3, ...), custom_call_target="tpu_custom_call" | custom-call | tf_op jit(solution)/shard_map/pallas_call | solution.py:537
  74.2 2.2 %shard_map.112 = (bf16[56,8192]{1,0:T(8,128)(2,1)}, f32[56,8192]{1,0:T(8,128)}, f32[56,8192]{1,0:T(8,128)}, bf16[2,3584]{1,0:T(2,128)(2,1)}) custom-call(bf16[56,8192]{1,0:T(8,128)(2,1)S(1)} %get-tuple-element.8.refs_0_, f32[56,8192]{1,0:T(8,128)S(1)} %get-tuple-element.9.refs_1_, f32[56,8192]{1,0:T(8,128)S(1)} %get-tuple-element.10.refs_2_, ...), custom_call_target="tpu_custom_call" | custom-call | tf_op jit(solution)/shard_map/pallas_call | solution.py:592
